TPU v7x, 256 devices: a whole 4x4x8 slice. The times are simulated.
256 devices in a mesh: row: 16 (over y, x_lo, core), col: 16 (over z, x_hi).
Axes of the slice: x: 4 (x_hi: 2, x_lo: 2; x = x_hi * 2 + x_lo), y: 4, z: 8, core: 2. Of those that a mesh axis runs over, the one named last changes fastest.
Arguments:
- density: float32 [128, 64, 1024], P('col', 'row'), may hold values from 0.3 to 3
- velocity: float32 [3, 128, 64, 1024], P(None, 'col', 'row'), may hold values from -2 to 2
- pressure: float32 [128, 64, 1024], P('col', 'row'), may hold values from 0.3 to 3
Outputs:
- state: float32 [5, 128, 64, 1024], P(None, 'col', 'row')
All inputs are finite; a program needn't handle non-finite values.
Results may differ from a plain program's by a relative error of at most 0.0003.
Values sent between devices are 32-bit elements; how exact they have to be, the bound alone decides.
No kernel may reach another device: no remote copies, remote signals or barrier semaphores. Data moves between devices by JAX's collectives and lax.ppermute only.
A program may use at most 64 MiB of HBM per device.

v0:
```python
import functools

import jax
import jax.numpy as jnp
from jax import lax
from jax.experimental import pallas as pl
from jax.experimental.pallas import tpu as pltpu
from jax.sharding import PartitionSpec as P

RIEMANN_ITERS = 3
GAMMA = 1.4
GM1 = 0.4
SHOCK = (GAMMA + 1.0) / (2.0 * GAMMA)
DTDX = 0.03
PRESSURE_FLOOR = 0.05
STAR_FLOOR = 0.1

NX, NY, NZ = 1024, 4, 8
TILES = NX // 128
HALO = 3
F32 = jnp.float32


def face_values(q0, q1, q2, q3):
    face = 7.0 / 12.0 * (q1 + q2) - 1.0 / 12.0 * (q0 + q3)
    return jnp.minimum(jnp.maximum(face, jnp.minimum(q1, q2)), jnp.maximum(q1, q2))


def cell_edges(q, face_left, face_right):
    dr = face_right - q
    dl = face_left - q
    br = 2.0 * jnp.abs(dr)
    bl = 2.0 * jnp.abs(dl)
    right = q + jnp.minimum(jnp.maximum(dr, -bl), bl)
    left = q + jnp.minimum(jnp.maximum(dl, -br), br)
    return left, right


def root(x):
    return x * lax.rsqrt(x)


def inverse(x):
    return 1.0 / x


def riemann(left, right):
    rl, ul, vl, wl, pl_ = left
    rr, ur, vr, wr, pr = right
    al = GAMMA * rl
    ar = GAMMA * rr
    cl = root(al * pl_)
    cr = root(ar * pr)
    jump = ul - ur
    floor = STAR_FLOOR * jnp.minimum(pl_, pr)
    sl = SHOCK * al
    sr = SHOCK * ar
    bl = (1.0 - SHOCK) * al * pl_
    br = (1.0 - SHOCK) * ar * pr

    def star(a, b):
        return jnp.maximum((b * (pl_ + a * jump) + a * pr) * inverse(a + b), floor)

    p = star(cl, cr)
    for _ in range(RIEMANN_ITERS):
        p = star(root(bl + sl * p), root(br + sr * p))
    a = root(bl + sl * p)
    b = root(br + sr * p)
    u = (a * ul + b * ur + (pl_ - pr)) * inverse(a + b)
    up = u > 0.0
    r = jnp.where(up, rl, rr)
    v = jnp.where(up, vl, vr)
    w = jnp.where(up, wl, wr)
    pu = jnp.where(up, pl_, pr)
    m = r * u
    energy = (1.0 / GM1) * pu + 0.5 * r * (u * u + v * v + w * w)
    return m, m * u + p, m * v, m * w, u * (energy + p)


def primitives(state, normal):
    rho = state[0]
    inv = inverse(rho)
    mom = [state[c] for c in normal]
    vel = [m * inv for m in mom]
    kinetic = 0.5 * (mom[0] * vel[0] + mom[1] * vel[1] + mom[2] * vel[2])
    pressure = jnp.maximum(GM1 * (state[4] - kinetic), PRESSURE_FLOOR)
    return [rho] + vel + [pressure]


def line_change(prims, cells):
    left, right = [], []
    for q in prims:
        n = q.shape[0]
        face = face_values(q[0 : n - 3], q[1 : n - 2], q[2 : n - 1], q[3:n])
        lo, hi = cell_edges(q[2 : n - 2], face[: n - 4], face[1:])
        left.append(hi[: cells + 1])
        right.append(lo[1:])
    flux = riemann(left, right)
    return [DTDX * (f[1:] - f[:-1]) for f in flux]


def x_line(tiles, store, m):
    lane = lax.broadcasted_iota(jnp.int32, (NZ, 128), 1)
    ring = len(tiles)

    def shift(row, k):
        turned = [pltpu.roll(q, (-k) % 128, axis=1) for q in row]
        if k > 0:
            return [jnp.where(lane < 128 - k, turned[t], turned[(t + 1) % ring]) for t in range(ring)]
        return [jnp.where(lane >= -k, turned[t], turned[t - 1]) for t in range(ring)]

    left, right = [], []
    for c in range(5):
        q = [p[c] for p in tiles]
        far = [shift(q, -1), q, shift(q, 1), shift(q, 2)]
        face = [face_values(*(f[t] for f in far)) for t in range(ring)]
        back = shift(face, -1)
        pairs = [cell_edges(q[t], back[t], face[t]) for t in range(ring)]
        left.append([p[1] for p in pairs])
        right.append(shift([p[0] for p in pairs], 1))
    flux = [riemann([l[t] for l in left], [r[t] for r in right]) for t in range(ring)]
    turned = [[pltpu.roll(f, 1, axis=1) for f in fs] for fs in flux]
    for t in range(m):
        rho, u, v, w, p = tiles[t]
        kinetic = 0.5 * rho * (u * u + v * v + w * w)
        state = (rho, rho * u, rho * v, rho * w, (1.0 / GM1) * p + kinetic)
        new = []
        for c in range(5):
            before = jnp.where(lane >= 1, turned[t][c], turned[t - 1][c])
            new.append(state[c] - DTDX * (flux[t][c] - before))
        store(t, new)


def x_kernel(start, m, q_ref, s_ref, f_ref, b_ref):
    lane = lax.broadcasted_iota(jnp.int32, (NZ, 128), 1)

    def line(y, carry):
        def load(t):
            tile = (start + t) % TILES
            return [q_ref[c, pl.ds(tile * NY + y, NZ, stride=TILES * NY), :] for c in range(5)]

        def store(t, new):
            for c in range(5):
                s_ref[c, y, t] = new[c]

        tiles = [load(t) for t in range(m)]
        if m < TILES:
            tiles.append([jnp.where(lane < 64, hi, lo) for hi, lo in zip(load(m), load(-1))])
        x_line(tiles, store, m)
        return carry

    lax.fori_loop(0, NY, line, 0)
    odd = lax.rem(lax.axis_index("row"), 2)
    f_ref[...] = s_ref[:, pl.ds(odd, HALO)]
    b_ref[...] = s_ref[:, pl.ds(1 - odd, HALO)]


def y_kernel(per, s_ref, f_in, b_in, t_ref, f_ref, b_ref):
    odd = lax.rem(lax.axis_index("row"), 2) == 1
    for t in range(per):
        full = [
            jnp.concatenate(
                [
                    jnp.where(odd, b_in[c, :, t], f_in[c, :, t]),
                    s_ref[c, :, t],
                    jnp.where(odd, f_in[c, :, t], b_in[c, :, t]),
                ],
                axis=0,
            )
            for c in range(5)
        ]
        change = line_change(primitives(full, (2, 1, 3)), NY)
        for c, k in enumerate((0, 2, 1, 3, 4)):
            new = full[c][HALO : HALO + NY] - change[k]
            for y in range(NY):
                t_ref[c, pl.ds(t * NY + y, NZ, stride=per * NY), :] = new[y]
    width = per * NY
    odd = lax.rem(lax.axis_index("col"), 2)
    for c in range(5):
        f_ref[c] = t_ref[c, pl.ds(pl.multiple_of(odd * (NZ - HALO) * width, 8), HALO * width)]
        b_ref[c] = t_ref[c, pl.ds(pl.multiple_of((1 - odd) * (NZ - HALO) * width, 8), HALO * width)]


def z_kernel(start, per, t_ref, b_in, f_in, _, o_hbm, o_ref, sems):
    width = per * NY
    odd = lax.rem(lax.axis_index("col"), 2) == 1

    def halo(even_ref, odd_ref, c, z, r):
        at = slice(z * width + r, z * width + r + 8)
        return jnp.where(odd, odd_ref[c, at], even_ref[c, at])

    copies = []
    for i, r in enumerate(range(0, width, 8)):
        full = [
            jnp.stack(
                [halo(f_in, b_in, c, z, r) for z in range(HALO)]
                + [t_ref[c, z * width + r : z * width + r + 8] for z in range(NZ)]
                + [halo(b_in, f_in, c, z, r) for z in range(HALO)]
            )
            for c in range(5)
        ]
        change = line_change(primitives(full, (3, 1, 2)), NZ)
        for c, k in enumerate((0, 2, 3, 1, 4)):
            new = full[c][HALO : HALO + NZ] - change[k]
            for z in range(NZ):
                o_ref[c, z, r : r + 8] = new[z]
        copies.append(
            pltpu.make_async_copy(
                o_ref.at[:, :, r : r + 8], o_hbm.at[:, :, start * NY + r : start * NY + r + 8], sems.at[i]
            )
        )
        copies[-1].start()
    for copy in copies:
        copy.wait()


def rows(a):
    lead = a.shape[:-3]
    a = jnp.swapaxes(a.reshape(*lead, NZ, NY, TILES, 128), -2, -3)
    return a.reshape(*lead, NZ * TILES * NY, 128)


def unrows(a):
    a = jnp.swapaxes(a.reshape(5, NZ, TILES, NY, 128), -2, -3)
    return a.reshape(5, NZ, NY, NX)


def cost(m, ops):
    cells = NZ * NY * 128 * m
    return pl.CostEstimate(flops=ops * cells, bytes_accessed=80 * cells, transcendentals=12 * cells)


def shape(*s):
    return jax.ShapeDtypeStruct(s, F32)


SMALL = pltpu.CompilerParams(vmem_limit_bytes=12 << 20)


CUTS = (0, 4, 8)


def local(density, velocity, pressure):
    n = lax.axis_size("row")
    inside = [(i, i ^ 1) for i in range(n)]
    across = [(i, (i + 1 if i % 2 else i - 1) % n) for i in range(n)]
    chunks = [(a, b - a) for a, b in zip(CUTS, CUTS[1:])]
    prims = jnp.concatenate([rows(density)[None], rows(velocity), rows(pressure)[None]])

    def x_sweep(start, m):
        return pl.pallas_call(
            functools.partial(x_kernel, start, m),
            out_shape=(shape(5, NY, m, NZ, 128), shape(5, HALO, m, NZ, 128), shape(5, HALO, m, NZ, 128)),
            compiler_params=SMALL,
            cost_estimate=cost(m, 1500),
            name=f"x{start}",
        )(prims)

    def y_sweep(start, m, s, f, b):
        w = m * NY
        return pl.pallas_call(
            functools.partial(y_kernel, m),
            out_shape=(shape(5, NZ * w, 128), shape(5, HALO * w, 128), shape(5, HALO * w, 128)),
            compiler_params=SMALL,
            cost_estimate=cost(m, 1000),
            name=f"y{start}",
        )(s, f, b)

    def z_sweep(start, m, t, f, b, out):
        w = m * NY
        first = out is None
        near = pl.BlockSpec(memory_space=pltpu.VMEM)
        far = pl.BlockSpec(memory_space=pl.ANY)
        kernel = functools.partial(z_kernel, start, m)
        return pl.pallas_call(
            (lambda t, b, f, *rest: kernel(t, b, f, None, *rest)) if first else kernel,
            in_specs=[near] * 3 + [far] * (not first),
            out_specs=far,
            out_shape=shape(5, NZ, TILES * NY, 128),
            scratch_shapes=[pltpu.VMEM((5, NZ, w, 128), F32), pltpu.SemaphoreType.DMA((w // 8,))],
            input_output_aliases={} if first else {3: 0},
            compiler_params=SMALL,
            cost_estimate=cost(m, 1000),
            name=f"z{start}",
        )(t, b, f, *([] if first else [out]))

    y_in = []
    for start, m in chunks:
        s, f, b = x_sweep(start, m)
        y_in.append((s, lax.ppermute(f, "row", across), lax.ppermute(b, "row", inside)))
    z_in = []
    for (start, m), args in zip(chunks, y_in):
        t, f, b = y_sweep(start, m, *args)
        z_in.append((t, lax.ppermute(b, "col", inside), lax.ppermute(f, "col", across)))
    out = None
    for (start, m), (t, b, f) in zip(chunks, z_in):
        out = z_sweep(start, m, t, f, b, out)
    return unrows(out)


def solution(mesh):
    placed = (P("col", "row", None), P(None, "col", "row", None), P("col", "row", None))
    return jax.shard_map(
        local, mesh=mesh, in_specs=placed, out_specs=P(None, "col", "row", None), check_vma=False
    )
```

profile of v0, /device:TPU:4, one launch (start us, length us, event | category | flops | bytes accessed | tf_op | source)
XLA Modules:
  0.0 33.6 jit_solution(11311968073378606518)
XLA Ops:
  0.0 1.1 %pad_maximum_fusion.q_ref = f32[5,256,128]{2,1,0:T(8,128)S(1)} fusion(f32[1,256,128]{2,1,0:T(8,128)} %bitcast.21, f32[3,256,128]{2,1,0:T(8,128)} %bitcast.20, f32[1,256,128]{2,1,0:T(8,128)} %bitcast.22), kind=kLoop, calls=%fused_computation | loop fusion | flops 327680 | bytes 1310720 | tf_op jit(solution)/shard_map/concatenate | solution.py:248
  1.1 2.2 %x0.1 = (f32[5,4,4,8,128]{4,3,2,1,0:T(8,128)S(1)}, f32[5,3,4,8,128]{4,3,2,1,0:T(8,128)S(1)}, f32[5,3,4,8,128]{4,3,2,1,0:T(8,128)S(1)}) custom-call(f32[5,256,128]{2,1,0:T(8,128)S(1)} %pad_maximum_fusion.q_ref), custom_call_target="tpu_custom_call" | custom-call | flops 24576000 | bytes 1310720 | tf_op jit(solution)/shard_map/x0/pallas_call | solution.py:251
  3.4 3.2 %collective-permute-start.4 = (f32[5,3,4,8,128]{4,3,2,1,0:T(8,128)S(1)}, f32[5,3,4,8,128]{4,3,2,1,0:T(8,128)S(1)}, u32[]{:S(2)}, u32[]{:S(2)}) collective-permute-start(f32[5,3,4,8,128]{4,3,2,1,0:T(8,128)S(1)} %get-tuple-element.24), channel_id=1, source_target_pairs={{0,240},{16,32},{32,16},{48,64},{64,48},{80,96},{96,80},{112,128},... | collective-permute-start | bytes 737288 | tf_op jit(solution)/shard_map/ppermute | solution.py:290
  6.5 0.0 collective-permute-start.5
  6.5 2.2 %x4.1 = (f32[5,4,4,8,128]{4,3,2,1,0:T(8,128)S(1)}, f32[5,3,4,8,128]{4,3,2,1,0:T(8,128)S(1)}, f32[5,3,4,8,128]{4,3,2,1,0:T(8,128)S(1)}) custom-call(f32[5,256,128]{2,1,0:T(8,128)S(1)} %pad_maximum_fusion.q_ref), custom_call_target="tpu_custom_call" | custom-call | flops 24576000 | bytes 1310720 | tf_op jit(solution)/shard_map/x4/pallas_call | solution.py:251
  8.8 1.0 %collective-permute-start = (f32[5,3,4,8,128]{4,3,2,1,0:T(8,128)S(1)}, f32[5,3,4,8,128]{4,3,2,1,0:T(8,128)S(1)}, u32[]{:S(2)}, u32[]{:S(2)}) collective-permute-start(f32[5,3,4,8,128]{4,3,2,1,0:T(8,128)S(1)} %get-tuple-element.18), channel_id=1, source_target_pairs={{0,240},{16,32},{32,16},{48,64},{64,48},{80,96},{96,80},{112,128},... | collective-permute-start | bytes 737288 | tf_op jit(solution)/shard_map/ppermute | solution.py:290
  9.8 0.0 collective-permute-start.1
  9.8 3.8 %collective-permute-done.4.f_in = f32[5,3,4,8,128]{4,3,2,1,0:T(8,128)S(1)} collective-permute-done((f32[5,3,4,8,128]{4,3,2,1,0:T(8,128)S(1)}, f32[5,3,4,8,128]{4,3,2,1,0:T(8,128)S(1)}, u32[]{:S(2)}, u32[]{:S(2)}) %collective-permute-start.4) | collective-permute-done | bytes 245792 | tf_op jit(solution)/shard_map/ppermute | solution.py:290
  13.6 0.0 collective-permute-done.5.b_in
  13.6 0.9 %y0.1 = (f32[5,128,128]{2,1,0:T(8,128)S(1)}, f32[5,48,128]{2,1,0:T(8,128)S(1)}, f32[5,48,128]{2,1,0:T(8,128)S(1)}) custom-call(f32[5,4,4,8,128]{4,3,2,1,0:T(8,128)S(1)} %get-tuple-element.23.s_ref, f32[5,3,4,8,128]{4,3,2,1,0:T(8,128)S(1)} %collective-permute-done.4.f_in, f32[5,3,4,8,128]{4,3,2,1,0:T(8,128)S(1)} %collective-permute-done.5.b_in), custom_call_target="tpu_custom_call" | custom-call | flops 16384000 | bytes 1310720 | tf_op jit(solution)/shard_map/y0/pallas_call | solution.py:261
  14.5 2.1 %collective-permute-start.6 = (f32[5,48,128]{2,1,0:T(8,128)S(1)}, f32[5,48,128]{2,1,0:T(8,128)S(1)}, u32[]{:S(2)}, u32[]{:S(2)}) collective-permute-start(f32[5,48,128]{2,1,0:T(8,128)S(1)} %get-tuple-element.27), channel_id=1, source_target_pairs={{0,1},{1,0},{2,3},{3,2},{4,5},{5,4},{6,7},{7,6},{8,9},{9,8},{10,11... | collective-permute-start | bytes 368648 | tf_op jit(solution)/shard_map/ppermute | solution.py:294
  16.6 2.9 %collective-permute-start.7 = (f32[5,48,128]{2,1,0:T(8,128)S(1)}, f32[5,48,128]{2,1,0:T(8,128)S(1)}, u32[]{:S(2)}, u32[]{:S(2)}) collective-permute-start(f32[5,48,128]{2,1,0:T(8,128)S(1)} %get-tuple-element.28), channel_id=1, source_target_pairs={{0,15},{1,2},{2,1},{3,4},{4,3},{5,6},{6,5},{7,8},{8,7},{9,10},{10,... | collective-permute-start | bytes 368648 | tf_op jit(solution)/shard_map/ppermute | solution.py:294
  19.5 0.0 collective-permute-done.f_in
  19.5 0.0 collective-permute-done.1.b_in
  19.5 0.9 %y4.1 = (f32[5,128,128]{2,1,0:T(8,128)S(1)}, f32[5,48,128]{2,1,0:T(8,128)S(1)}, f32[5,48,128]{2,1,0:T(8,128)S(1)}) custom-call(f32[5,4,4,8,128]{4,3,2,1,0:T(8,128)S(1)} %get-tuple-element.17.s_ref, f32[5,3,4,8,128]{4,3,2,1,0:T(8,128)S(1)} %collective-permute-done.f_in, f32[5,3,4,8,128]{4,3,2,1,0:T(8,128)S(1)} %collective-permute-done.1.b_in), custom_call_target="tpu_custom_call" | custom-call | flops 16384000 | bytes 1310720 | tf_op jit(solution)/shard_map/y4/pallas_call | solution.py:261
  20.4 4.5 %collective-permute-start.2 = (f32[5,48,128]{2,1,0:T(8,128)S(1)}, f32[5,48,128]{2,1,0:T(8,128)S(1)}, u32[]{:S(2)}, u32[]{:S(2)}) collective-permute-start(f32[5,48,128]{2,1,0:T(8,128)S(1)} %get-tuple-element.21), channel_id=1, source_target_pairs={{0,1},{1,0},{2,3},{3,2},{4,5},{5,4},{6,7},{7,6},{8,9},{9,8},{10,11... | collective-permute-start | bytes 368648 | tf_op jit(solution)/shard_map/ppermute | solution.py:294
  24.9 0.5 %collective-permute-start.3 = (f32[5,48,128]{2,1,0:T(8,128)S(1)}, f32[5,48,128]{2,1,0:T(8,128)S(1)}, u32[]{:S(2)}, u32[]{:S(2)}) collective-permute-start(f32[5,48,128]{2,1,0:T(8,128)S(1)} %get-tuple-element.22), channel_id=1, source_target_pairs={{0,15},{1,2},{2,1},{3,4},{4,3},{5,6},{6,5},{7,8},{8,7},{9,10},{10,... | collective-permute-start | bytes 368648 | tf_op jit(solution)/shard_map/ppermute | solution.py:294
  25.4 0.0 collective-permute-done.6.b
  25.4 0.0 collective-permute-done.7.f
  25.4 1.4 %z0.1._ = f32[5,8,32,128]{3,2,1,0:T(8,128)} custom-call(f32[5,128,128]{2,1,0:T(8,128)S(1)} %get-tuple-element.26.t, f32[5,48,128]{2,1,0:T(8,128)S(1)} %collective-permute-done.6.b, f32[5,48,128]{2,1,0:T(8,128)S(1)} %collective-permute-done.7.f), custom_call_target="tpu_custom_call" | custom-call | flops 16384000 | bytes 1310720 | tf_op jit(solution)/shard_map/z0/pallas_call | solution.py:275
  26.8 2.3 %collective-permute-done.2.b_in = f32[5,48,128]{2,1,0:T(8,128)S(1)} collective-permute-done((f32[5,48,128]{2,1,0:T(8,128)S(1)}, f32[5,48,128]{2,1,0:T(8,128)S(1)}, u32[]{:S(2)}, u32[]{:S(2)}) %collective-permute-start.2) | collective-permute-done | bytes 122912 | tf_op jit(solution)/shard_map/ppermute | solution.py:294
  29.1 3.1 %collective-permute-done.3.f_in = f32[5,48,128]{2,1,0:T(8,128)S(1)} collective-permute-done((f32[5,48,128]{2,1,0:T(8,128)S(1)}, f32[5,48,128]{2,1,0:T(8,128)S(1)}, u32[]{:S(2)}, u32[]{:S(2)}) %collective-permute-start.3) | collective-permute-done | bytes 122912 | tf_op jit(solution)/shard_map/ppermute | solution.py:294
  32.2 1.4 %z4.1 = f32[5,8,32,128]{3,2,1,0:T(8,128)} custom-call(f32[5,128,128]{2,1,0:T(8,128)S(1)} %get-tuple-element.20.t_ref, f32[5,48,128]{2,1,0:T(8,128)S(1)} %collective-permute-done.2.b_in, f32[5,48,128]{2,1,0:T(8,128)S(1)} %collective-permute-done.3.f_in, f32[5,8,32,128]{3,2,1,0:T(8,128)} %z0.1._), custom_call_target="tpu_custom_call", output_to_operand_aliasing={{}: (3, {})} | custom-call | flops 16384000 | bytes 1310720 | tf_op jit(solution)/shard_map/z4/pallas_call | solution.py:275
Async XLA Ops:
  3.4 10.2 %collective-permute-start.4 = (f32[5,3,4,8,128]{4,3,2,1,0:T(8,128)S(1)}, f32[5,3,4,8,128]{4,3,2,1,0:T(8,128)S(1)}, u32[]{:S(2)}, u32[]{:S(2)}) collective-permute-start(f32[5,3,4,8,128]{4,3,2,1,0:T(8,128)S(1)} %get-tuple-element.24), channel_id=1, source_target_pairs={{0,240},{16,32},{32,16},{48,64},{64,48},{80,96},{96,80},{112,128},... | collective-permute-start | bytes 737288 | tf_op jit(solution)/shard_map/ppermute | solution.py:290
  6.5 7.0 %collective-permute-start.5 = (f32[5,3,4,8,128]{4,3,2,1,0:T(8,128)S(1)}, f32[5,3,4,8,128]{4,3,2,1,0:T(8,128)S(1)}, u32[]{:S(2)}, u32[]{:S(2)}) collective-permute-start(f32[5,3,4,8,128]{4,3,2,1,0:T(8,128)S(1)} %get-tuple-element.25), channel_id=1, source_target_pairs={{0,16},{16,0},{32,48},{48,32},{64,80},{80,64},{96,112},{112,96},{1... | collective-permute-start | bytes 737288 | tf_op jit(solution)/shard_map/ppermute | solution.py:290
  8.8 10.7 %collective-permute-start = (f32[5,3,4,8,128]{4,3,2,1,0:T(8,128)S(1)}, f32[5,3,4,8,128]{4,3,2,1,0:T(8,128)S(1)}, u32[]{:S(2)}, u32[]{:S(2)}) collective-permute-start(f32[5,3,4,8,128]{4,3,2,1,0:T(8,128)S(1)} %get-tuple-element.18), channel_id=1, source_target_pairs={{0,240},{16,32},{32,16},{48,64},{64,48},{80,96},{96,80},{112,128},... | collective-permute-start | bytes 737288 | tf_op jit(solution)/shard_map/ppermute | solution.py:290
  9.8 9.7 %collective-permute-start.1 = (f32[5,3,4,8,128]{4,3,2,1,0:T(8,128)S(1)}, f32[5,3,4,8,128]{4,3,2,1,0:T(8,128)S(1)}, u32[]{:S(2)}, u32[]{:S(2)}) collective-permute-start(f32[5,3,4,8,128]{4,3,2,1,0:T(8,128)S(1)} %get-tuple-element.19), channel_id=1, source_target_pairs={{0,16},{16,0},{32,48},{48,32},{64,80},{80,64},{96,112},{112,96},{1... | collective-permute-start | bytes 737288 | tf_op jit(solution)/shard_map/ppermute | solution.py:290
  14.5 10.9 %collective-permute-start.6 = (f32[5,48,128]{2,1,0:T(8,128)S(1)}, f32[5,48,128]{2,1,0:T(8,128)S(1)}, u32[]{:S(2)}, u32[]{:S(2)}) collective-permute-start(f32[5,48,128]{2,1,0:T(8,128)S(1)} %get-tuple-element.27), channel_id=1, source_target_pairs={{0,1},{1,0},{2,3},{3,2},{4,5},{5,4},{6,7},{7,6},{8,9},{9,8},{10,11... | collective-permute-start | bytes 368648 | tf_op jit(solution)/shard_map/ppermute | solution.py:294
  16.6 8.8 %collective-permute-start.7 = (f32[5,48,128]{2,1,0:T(8,128)S(1)}, f32[5,48,128]{2,1,0:T(8,128)S(1)}, u32[]{:S(2)}, u32[]{:S(2)}) collective-permute-start(f32[5,48,128]{2,1,0:T(8,128)S(1)} %get-tuple-element.28), channel_id=1, source_target_pairs={{0,15},{1,2},{2,1},{3,4},{4,3},{5,6},{6,5},{7,8},{8,7},{9,10},{10,... | collective-permute-start | bytes 368648 | tf_op jit(solution)/shard_map/ppermute | solution.py:294
  20.4 8.7 %collective-permute-start.2 = (f32[5,48,128]{2,1,0:T(8,128)S(1)}, f32[5,48,128]{2,1,0:T(8,128)S(1)}, u32[]{:S(2)}, u32[]{:S(2)}) collective-permute-start(f32[5,48,128]{2,1,0:T(8,128)S(1)} %get-tuple-element.21), channel_id=1, source_target_pairs={{0,1},{1,0},{2,3},{3,2},{4,5},{5,4},{6,7},{7,6},{8,9},{9,8},{10,11... | collective-permute-start | bytes 368648 | tf_op jit(solution)/shard_map/ppermute | solution.py:294
  24.9 7.3 %collective-permute-start.3 = (f32[5,48,128]{2,1,0:T(8,128)S(1)}, f32[5,48,128]{2,1,0:T(8,128)S(1)}, u32[]{:S(2)}, u32[]{:S(2)}) collective-permute-start(f32[5,48,128]{2,1,0:T(8,128)S(1)} %get-tuple-element.22), channel_id=1, source_target_pairs={{0,15},{1,2},{2,1},{3,4},{4,3},{5,6},{6,5},{7,8},{8,7},{9,10},{10,... | collective-permute-start | bytes 368648 | tf_op jit(solution)/shard_map/ppermute | solution.py:294
where the time goes:
time: 33.7 us; the launch traced here: 33.6 us
  starting transfers between devices  14.1 us (42%)
  waiting for transfers between devices  9.18 us (27%)
  Pallas kernels  9.06 us (27%)
  other arithmetic  1.13 us (3%)
    ppermute x2, starting transfers between devices, local(): lax.ppermute(b, 'col', inside)  6.57 us
    pallas_call x2, Pallas kernels, x_sweep(): pl.pallas_call(functools.partial(x_kernel, start, m), out_shape=(shape(5,...  4.44 us
    ppermute x2, starting transfers between devices, local(): lax.ppermute(f, 'row', across)  4.2 us
    ppermute x2, waiting for transfers between devices, local(): lax.ppermute(f, 'row', across)  3.76 us
    ppermute x2, starting transfers between devices, local(): lax.ppermute(f, 'col', across)  3.37 us
    ppermute x2, waiting for transfers between devices, local(): lax.ppermute(f, 'col', across)  3.11 us
    pallas_call x2, Pallas kernels, z_sweep(): pl.pallas_call((lambda t, b, f, *rest: kernel(t, b, f, None, *rest)) if f...  2.75 us
    ppermute x2, waiting for transfers between devices, local(): lax.ppermute(b, 'col', inside)  2.31 us
  transfers between devices with their start and end apart: 8, of which 3 were waited for; matrix products, arithmetic and copies ran while one was open for 0% of the time, Pallas kernels for 16%

commit v1 on v0

--- a/solution.py
+++ b/solution.py
@@ -149,7 +149,7 @@
         x_line(tiles, store, m)
         return carry
 
-    lax.fori_loop(0, NY, line, 0)
+    lax.fori_loop(0, NY, line, 0, unroll=2)
     odd = lax.rem(lax.axis_index("row"), 2)
     f_ref[...] = s_ref[:, pl.ds(odd, HALO)]
     b_ref[...] = s_ref[:, pl.ds(1 - odd, HALO)]

time: 33.7 us -> 33 us (0.979)
  Pallas kernels: 9.06 us -> 7.62 us
  waiting for transfers between devices: 9.18 us -> 9.9 us
    pallas_call x2, Pallas kernels: 4.44 us -> 2.99 us  [x_sweep(): pl.pallas_call(functools.partial(x_kernel, start, m), out_shape=(shape(5,...]
    ppermute x2, waiting for transfers between devices: 3.76 us -> 4.48 us  [local(): lax.ppermute(f, 'row', across)]
    ppermute x2, starting transfers between devices: 3.37 us -> 2.83 us  [local(): lax.ppermute(f, 'col', across)]
    ppermute x2, starting transfers between devices: 6.57 us -> 7.12 us  [local(): lax.ppermute(b, 'col', inside)]
  transfers between devices with their start and end apart: 8 -> 8, of which waited for: 3 -> 3; matrix products, arithmetic and copies ran while one was open for 0% -> 0% of each run, Pallas kernels for 16% -> 14%
where the time goes in v1:
time: 33 us; the launch traced here: 32.8 us
  starting transfers between devices  14.1 us (43%)
  waiting for transfers between devices  9.9 us (30%)
  Pallas kernels  7.62 us (23%)
  other arithmetic  1.13 us (3%)
    ppermute x2, starting transfers between devices, local(): lax.ppermute(b, 'col', inside)  7.12 us
    ppermute x2, waiting for transfers between devices, local(): lax.ppermute(f, 'row', across)  4.48 us
    ppermute x2, starting transfers between devices, local(): lax.ppermute(f, 'row', across)  4.2 us
    ppermute x2, waiting for transfers between devices, local(): lax.ppermute(f, 'col', across)  3.11 us
    pallas_call x2, Pallas kernels, x_sweep(): pl.pallas_call(functools.partial(x_kernel, start, m), out_shape=(shape(5,...  2.99 us
    ppermute x2, starting transfers between devices, local(): lax.ppermute(f, 'col', across)  2.83 us
    pallas_call x2, Pallas kernels, z_sweep(): pl.pallas_call((lambda t, b, f, *rest: kernel(t, b, f, None, *rest)) if f...  2.75 us
    ppermute x2, waiting for transfers between devices, local(): lax.ppermute(b, 'col', inside)  2.31 us
  transfers between devices with their start and end apart: 8, of which 3 were waited for; matrix products, arithmetic and copies ran while one was open for 0% of the time, Pallas kernels for 14%

profile of v1, /device:TPU:4, one launch (start us, length us, event | category | flops | bytes accessed | tf_op | source)
XLA Modules:
  0.0 32.8 jit_solution(8645713765268787221)
XLA Ops:
  0.0 1.1 %pad_maximum_fusion.q_ref = f32[5,256,128]{2,1,0:T(8,128)S(1)} fusion(f32[1,256,128]{2,1,0:T(8,128)} %bitcast.21, f32[3,256,128]{2,1,0:T(8,128)} %bitcast.20, f32[1,256,128]{2,1,0:T(8,128)} %bitcast.22), kind=kLoop, calls=%fused_computation | loop fusion | flops 327680 | bytes 1310720 | tf_op jit(solution)/shard_map/concatenate | solution.py:248
  1.1 1.5 %x0.1 = (f32[5,4,4,8,128]{4,3,2,1,0:T(8,128)S(1)}, f32[5,3,4,8,128]{4,3,2,1,0:T(8,128)S(1)}, f32[5,3,4,8,128]{4,3,2,1,0:T(8,128)S(1)}) custom-call(f32[5,256,128]{2,1,0:T(8,128)S(1)} %pad_maximum_fusion.q_ref), custom_call_target="tpu_custom_call" | custom-call | flops 24576000 | bytes 1310720 | tf_op jit(solution)/shard_map/x0/pallas_call | solution.py:251
  2.6 3.2 %collective-permute-start.4 = (f32[5,3,4,8,128]{4,3,2,1,0:T(8,128)S(1)}, f32[5,3,4,8,128]{4,3,2,1,0:T(8,128)S(1)}, u32[]{:S(2)}, u32[]{:S(2)}) collective-permute-start(f32[5,3,4,8,128]{4,3,2,1,0:T(8,128)S(1)} %get-tuple-element.24), channel_id=1, source_target_pairs={{0,240},{16,32},{32,16},{48,64},{64,48},{80,96},{96,80},{112,128},... | collective-permute-start | bytes 737288 | tf_op jit(solution)/shard_map/ppermute | solution.py:290
  5.8 0.0 collective-permute-start.5
  5.8 1.5 %x4.1 = (f32[5,4,4,8,128]{4,3,2,1,0:T(8,128)S(1)}, f32[5,3,4,8,128]{4,3,2,1,0:T(8,128)S(1)}, f32[5,3,4,8,128]{4,3,2,1,0:T(8,128)S(1)}) custom-call(f32[5,256,128]{2,1,0:T(8,128)S(1)} %pad_maximum_fusion.q_ref), custom_call_target="tpu_custom_call" | custom-call | flops 24576000 | bytes 1310720 | tf_op jit(solution)/shard_map/x4/pallas_call | solution.py:251
  7.3 1.0 %collective-permute-start = (f32[5,3,4,8,128]{4,3,2,1,0:T(8,128)S(1)}, f32[5,3,4,8,128]{4,3,2,1,0:T(8,128)S(1)}, u32[]{:S(2)}, u32[]{:S(2)}) collective-permute-start(f32[5,3,4,8,128]{4,3,2,1,0:T(8,128)S(1)} %get-tuple-element.18), channel_id=1, source_target_pairs={{0,240},{16,32},{32,16},{48,64},{64,48},{80,96},{96,80},{112,128},... | collective-permute-start | bytes 737288 | tf_op jit(solution)/shard_map/ppermute | solution.py:290
  8.4 0.0 collective-permute-start.1
  8.4 4.5 %collective-permute-done.4.f_in = f32[5,3,4,8,128]{4,3,2,1,0:T(8,128)S(1)} collective-permute-done((f32[5,3,4,8,128]{4,3,2,1,0:T(8,128)S(1)}, f32[5,3,4,8,128]{4,3,2,1,0:T(8,128)S(1)}, u32[]{:S(2)}, u32[]{:S(2)}) %collective-permute-start.4) | collective-permute-done | bytes 245792 | tf_op jit(solution)/shard_map/ppermute | solution.py:290
  12.8 0.0 collective-permute-done.5.b_in
  12.8 0.9 %y0.1 = (f32[5,128,128]{2,1,0:T(8,128)S(1)}, f32[5,48,128]{2,1,0:T(8,128)S(1)}, f32[5,48,128]{2,1,0:T(8,128)S(1)}) custom-call(f32[5,4,4,8,128]{4,3,2,1,0:T(8,128)S(1)} %get-tuple-element.23.s_ref, f32[5,3,4,8,128]{4,3,2,1,0:T(8,128)S(1)} %collective-permute-done.4.f_in, f32[5,3,4,8,128]{4,3,2,1,0:T(8,128)S(1)} %collective-permute-done.5.b_in), custom_call_target="tpu_custom_call" | custom-call | flops 16384000 | bytes 1310720 | tf_op jit(solution)/shard_map/y0/pallas_call | solution.py:261
  13.8 2.6 %collective-permute-start.6 = (f32[5,48,128]{2,1,0:T(8,128)S(1)}, f32[5,48,128]{2,1,0:T(8,128)S(1)}, u32[]{:S(2)}, u32[]{:S(2)}) collective-permute-start(f32[5,48,128]{2,1,0:T(8,128)S(1)} %get-tuple-element.27), channel_id=1, source_target_pairs={{0,1},{1,0},{2,3},{3,2},{4,5},{5,4},{6,7},{7,6},{8,9},{9,8},{10,11... | collective-permute-start | bytes 368648 | tf_op jit(solution)/shard_map/ppermute | solution.py:294
  16.4 2.3 %collective-permute-start.7 = (f32[5,48,128]{2,1,0:T(8,128)S(1)}, f32[5,48,128]{2,1,0:T(8,128)S(1)}, u32[]{:S(2)}, u32[]{:S(2)}) collective-permute-start(f32[5,48,128]{2,1,0:T(8,128)S(1)} %get-tuple-element.28), channel_id=1, source_target_pairs={{0,15},{1,2},{2,1},{3,4},{4,3},{5,6},{6,5},{7,8},{8,7},{9,10},{10,... | collective-permute-start | bytes 368648 | tf_op jit(solution)/shard_map/ppermute | solution.py:294
  18.7 0.0 collective-permute-done.f_in
  18.8 0.0 collective-permute-done.1.b_in
  18.8 0.9 %y4.1 = (f32[5,128,128]{2,1,0:T(8,128)S(1)}, f32[5,48,128]{2,1,0:T(8,128)S(1)}, f32[5,48,128]{2,1,0:T(8,128)S(1)}) custom-call(f32[5,4,4,8,128]{4,3,2,1,0:T(8,128)S(1)} %get-tuple-element.17.s_ref, f32[5,3,4,8,128]{4,3,2,1,0:T(8,128)S(1)} %collective-permute-done.f_in, f32[5,3,4,8,128]{4,3,2,1,0:T(8,128)S(1)} %collective-permute-done.1.b_in), custom_call_target="tpu_custom_call" | custom-call | flops 16384000 | bytes 1310720 | tf_op jit(solution)/shard_map/y4/pallas_call | solution.py:261
  19.7 4.5 %collective-permute-start.2 = (f32[5,48,128]{2,1,0:T(8,128)S(1)}, f32[5,48,128]{2,1,0:T(8,128)S(1)}, u32[]{:S(2)}, u32[]{:S(2)}) collective-permute-start(f32[5,48,128]{2,1,0:T(8,128)S(1)} %get-tuple-element.21), channel_id=1, source_target_pairs={{0,1},{1,0},{2,3},{3,2},{4,5},{5,4},{6,7},{7,6},{8,9},{9,8},{10,11... | collective-permute-start | bytes 368648 | tf_op jit(solution)/shard_map/ppermute | solution.py:294
  24.2 0.5 %collective-permute-start.3 = (f32[5,48,128]{2,1,0:T(8,128)S(1)}, f32[5,48,128]{2,1,0:T(8,128)S(1)}, u32[]{:S(2)}, u32[]{:S(2)}) collective-permute-start(f32[5,48,128]{2,1,0:T(8,128)S(1)} %get-tuple-element.22), channel_id=1, source_target_pairs={{0,15},{1,2},{2,1},{3,4},{4,3},{5,6},{6,5},{7,8},{8,7},{9,10},{10,... | collective-permute-start | bytes 368648 | tf_op jit(solution)/shard_map/ppermute | solution.py:294
  24.7 0.0 collective-permute-done.6.b
  24.7 0.0 collective-permute-done.7.f
  24.7 1.4 %z0.1._ = f32[5,8,32,128]{3,2,1,0:T(8,128)} custom-call(f32[5,128,128]{2,1,0:T(8,128)S(1)} %get-tuple-element.26.t, f32[5,48,128]{2,1,0:T(8,128)S(1)} %collective-permute-done.6.b, f32[5,48,128]{2,1,0:T(8,128)S(1)} %collective-permute-done.7.f), custom_call_target="tpu_custom_call" | custom-call | flops 16384000 | bytes 1310720 | tf_op jit(solution)/shard_map/z0/pallas_call | solution.py:275
  26.1 2.3 %collective-permute-done.2.b_in = f32[5,48,128]{2,1,0:T(8,128)S(1)} collective-permute-done((f32[5,48,128]{2,1,0:T(8,128)S(1)}, f32[5,48,128]{2,1,0:T(8,128)S(1)}, u32[]{:S(2)}, u32[]{:S(2)}) %collective-permute-start.2) | collective-permute-done | bytes 122912 | tf_op jit(solution)/shard_map/ppermute | solution.py:294
  28.4 3.1 %collective-permute-done.3.f_in = f32[5,48,128]{2,1,0:T(8,128)S(1)} collective-permute-done((f32[5,48,128]{2,1,0:T(8,128)S(1)}, f32[5,48,128]{2,1,0:T(8,128)S(1)}, u32[]{:S(2)}, u32[]{:S(2)}) %collective-permute-start.3) | collective-permute-done | bytes 122912 | tf_op jit(solution)/shard_map/ppermute | solution.py:294
  31.5 1.4 %z4.1 = f32[5,8,32,128]{3,2,1,0:T(8,128)} custom-call(f32[5,128,128]{2,1,0:T(8,128)S(1)} %get-tuple-element.20.t_ref, f32[5,48,128]{2,1,0:T(8,128)S(1)} %collective-permute-done.2.b_in, f32[5,48,128]{2,1,0:T(8,128)S(1)} %collective-permute-done.3.f_in, f32[5,8,32,128]{3,2,1,0:T(8,128)} %z0.1._), custom_call_target="tpu_custom_call", output_to_operand_aliasing={{}: (3, {})} | custom-call | flops 16384000 | bytes 1310720 | tf_op jit(solution)/shard_map/z4/pallas_call | solution.py:275
Async XLA Ops:
  2.6 10.2 %collective-permute-start.4 = (f32[5,3,4,8,128]{4,3,2,1,0:T(8,128)S(1)}, f32[5,3,4,8,128]{4,3,2,1,0:T(8,128)S(1)}, u32[]{:S(2)}, u32[]{:S(2)}) collective-permute-start(f32[5,3,4,8,128]{4,3,2,1,0:T(8,128)S(1)} %get-tuple-element.24), channel_id=1, source_target_pairs={{0,240},{16,32},{32,16},{48,64},{64,48},{80,96},{96,80},{112,128},... | collective-permute-start | bytes 737288 | tf_op jit(solution)/shard_map/ppermute | solution.py:290
  5.8 7.0 %collective-permute-start.5 = (f32[5,3,4,8,128]{4,3,2,1,0:T(8,128)S(1)}, f32[5,3,4,8,128]{4,3,2,1,0:T(8,128)S(1)}, u32[]{:S(2)}, u32[]{:S(2)}) collective-permute-start(f32[5,3,4,8,128]{4,3,2,1,0:T(8,128)S(1)} %get-tuple-element.25), channel_id=1, source_target_pairs={{0,16},{16,0},{32,48},{48,32},{64,80},{80,64},{96,112},{112,96},{1... | collective-permute-start | bytes 737288 | tf_op jit(solution)/shard_map/ppermute | solution.py:290
  7.3 11.4 %collective-permute-start = (f32[5,3,4,8,128]{4,3,2,1,0:T(8,128)S(1)}, f32[5,3,4,8,128]{4,3,2,1,0:T(8,128)S(1)}, u32[]{:S(2)}, u32[]{:S(2)}) collective-permute-start(f32[5,3,4,8,128]{4,3,2,1,0:T(8,128)S(1)} %get-tuple-element.18), channel_id=1, source_target_pairs={{0,240},{16,32},{32,16},{48,64},{64,48},{80,96},{96,80},{112,128},... | collective-permute-start | bytes 737288 | tf_op jit(solution)/shard_map/ppermute | solution.py:290
  8.4 10.4 %collective-permute-start.1 = (f32[5,3,4,8,128]{4,3,2,1,0:T(8,128)S(1)}, f32[5,3,4,8,128]{4,3,2,1,0:T(8,128)S(1)}, u32[]{:S(2)}, u32[]{:S(2)}) collective-permute-start(f32[5,3,4,8,128]{4,3,2,1,0:T(8,128)S(1)} %get-tuple-element.19), channel_id=1, source_target_pairs={{0,16},{16,0},{32,48},{48,32},{64,80},{80,64},{96,112},{112,96},{1... | collective-permute-start | bytes 737288 | tf_op jit(solution)/shard_map/ppermute | solution.py:290
  13.8 10.9 %collective-permute-start.6 = (f32[5,48,128]{2,1,0:T(8,128)S(1)}, f32[5,48,128]{2,1,0:T(8,128)S(1)}, u32[]{:S(2)}, u32[]{:S(2)}) collective-permute-start(f32[5,48,128]{2,1,0:T(8,128)S(1)} %get-tuple-element.27), channel_id=1, source_target_pairs={{0,1},{1,0},{2,3},{3,2},{4,5},{5,4},{6,7},{7,6},{8,9},{9,8},{10,11... | collective-permute-start | bytes 368648 | tf_op jit(solution)/shard_map/ppermute | solution.py:294
  16.4 8.3 %collective-permute-start.7 = (f32[5,48,128]{2,1,0:T(8,128)S(1)}, f32[5,48,128]{2,1,0:T(8,128)S(1)}, u32[]{:S(2)}, u32[]{:S(2)}) collective-permute-start(f32[5,48,128]{2,1,0:T(8,128)S(1)} %get-tuple-element.28), channel_id=1, source_target_pairs={{0,15},{1,2},{2,1},{3,4},{4,3},{5,6},{6,5},{7,8},{8,7},{9,10},{10,... | collective-permute-start | bytes 368648 | tf_op jit(solution)/shard_map/ppermute | solution.py:294
  19.7 8.7 %collective-permute-start.2 = (f32[5,48,128]{2,1,0:T(8,128)S(1)}, f32[5,48,128]{2,1,0:T(8,128)S(1)}, u32[]{:S(2)}, u32[]{:S(2)}) collective-permute-start(f32[5,48,128]{2,1,0:T(8,128)S(1)} %get-tuple-element.21), channel_id=1, source_target_pairs={{0,1},{1,0},{2,3},{3,2},{4,5},{5,4},{6,7},{7,6},{8,9},{9,8},{10,11... | collective-permute-start | bytes 368648 | tf_op jit(solution)/shard_map/ppermute | solution.py:294
  24.2 7.3 %collective-permute-start.3 = (f32[5,48,128]{2,1,0:T(8,128)S(1)}, f32[5,48,128]{2,1,0:T(8,128)S(1)}, u32[]{:S(2)}, u32[]{:S(2)}) collective-permute-start(f32[5,48,128]{2,1,0:T(8,128)S(1)} %get-tuple-element.22), channel_id=1, source_target_pairs={{0,15},{1,2},{2,1},{3,4},{4,3},{5,6},{6,5},{7,8},{8,7},{9,10},{10,... | collective-permute-start | bytes 368648 | tf_op jit(solution)/shard_map/ppermute | solution.py:294

commit v2 on v1

--- a/solution.py
+++ b/solution.py
@@ -99,57 +99,47 @@
     return [DTDX * (f[1:] - f[:-1]) for f in flux]
 
 
-def x_line(tiles, store, m):
-    lane = lax.broadcasted_iota(jnp.int32, (NZ, 128), 1)
-    ring = len(tiles)
-
-    def shift(row, k):
-        turned = [pltpu.roll(q, (-k) % 128, axis=1) for q in row]
-        if k > 0:
-            return [jnp.where(lane < 128 - k, turned[t], turned[(t + 1) % ring]) for t in range(ring)]
-        return [jnp.where(lane >= -k, turned[t], turned[t - 1]) for t in range(ring)]
-
-    left, right = [], []
+def x_kernel(start, m, q_ref, s_ref, f_ref, b_ref, work, done):
+    rows_per = NY * NZ
+    lanes = m * rows_per
+    lane = lax.broadcasted_iota(jnp.int32, (8, lanes), 1)
+
+    def tile(c, t):
+        at = (start + t) % TILES * NY
+        return [q_ref[c, pl.ds(at + y, NZ, stride=TILES * NY), :] for y in range(NY)]
+
     for c in range(5):
-        q = [p[c] for p in tiles]
-        far = [shift(q, -1), q, shift(q, 1), shift(q, 2)]
-        face = [face_values(*(f[t] for f in far)) for t in range(ring)]
-        back = shift(face, -1)
-        pairs = [cell_edges(q[t], back[t], face[t]) for t in range(ring)]
-        left.append([p[1] for p in pairs])
-        right.append(shift([p[0] for p in pairs], 1))
-    flux = [riemann([l[t] for l in left], [r[t] for r in right]) for t in range(ring)]
-    turned = [[pltpu.roll(f, 1, axis=1) for f in fs] for fs in flux]
-    for t in range(m):
-        rho, u, v, w, p = tiles[t]
-        kinetic = 0.5 * rho * (u * u + v * v + w * w)
-        state = (rho, rho * u, rho * v, rho * w, (1.0 / GM1) * p + kinetic)
-        new = []
-        for c in range(5):
-            before = jnp.where(lane >= 1, turned[t][c], turned[t - 1][c])
-            new.append(state[c] - DTDX * (flux[t][c] - before))
-        store(t, new)
-
-
-def x_kernel(start, m, q_ref, s_ref, f_ref, b_ref):
-    lane = lax.broadcasted_iota(jnp.int32, (NZ, 128), 1)
-
-    def line(y, carry):
-        def load(t):
-            tile = (start + t) % TILES
-            return [q_ref[c, pl.ds(tile * NY + y, NZ, stride=TILES * NY), :] for c in range(5)]
-
-        def store(t, new):
+        own = jnp.concatenate([r for t in range(m) for r in tile(c, t)], axis=0).T
+        before, behind = tile(c, -1), tile(c, m)
+        edge = jnp.concatenate(before * (m - 1) + behind, axis=0).T
+        work[c, 8:136] = own
+        work[c, 0:8] = jnp.where(lane < rows_per, edge[120:], pltpu.roll(own[120:], rows_per, axis=1))
+        work[c, 136:144] = jnp.where(lane >= lanes - rows_per, edge[:8], pltpu.roll(own[:8], lanes - rows_per, axis=1))
+    cells = 16
+    prims, faces, edges, flux = [], [], [], None
+    for k in range(cells + 2 * HALO):
+        prims.append([work[c, pl.ds(8 + k - HALO, 8, stride=cells), :] for c in range(5)])
+        if k < 3:
+            continue
+        faces.append([face_values(*(prims[k - 3 + i][c] for i in range(4))) for c in range(5)])
+        if k < 4:
+            continue
+        edges.append([cell_edges(prims[k - 2][c], faces[-2][c], faces[-1][c]) for c in range(5)])
+        if k < 5:
+            continue
+        now = riemann([e[1] for e in edges[-2]], [e[0] for e in edges[-1]])
+        if k > 5:
+            rho, u, v, w, p = prims[k - 3]
+            kinetic = 0.5 * rho * (u * u + v * v + w * w)
+            state = (rho, rho * u, rho * v, rho * w, (1.0 / GM1) * p + kinetic)
             for c in range(5):
-                s_ref[c, y, t] = new[c]
-
-        tiles = [load(t) for t in range(m)]
-        if m < TILES:
-            tiles.append([jnp.where(lane < 64, hi, lo) for hi, lo in zip(load(m), load(-1))])
-        x_line(tiles, store, m)
-        return carry
-
-    lax.fori_loop(0, NY, line, 0, unroll=2)
+                done[c, pl.ds(k - 6, 8, stride=cells), :] = state[c] - DTDX * (now[c] - flux[c])
+        flux = now
+    for c in range(5):
+        back = done[c].T
+        for t in range(m):
+            for y in range(NY):
+                s_ref[c, y, t] = back[(t * NY + y) * NZ : (t * NY + y + 1) * NZ]
     odd = lax.rem(lax.axis_index("row"), 2)
     f_ref[...] = s_ref[:, pl.ds(odd, HALO)]
     b_ref[...] = s_ref[:, pl.ds(1 - odd, HALO)]
@@ -252,19 +242,22 @@
             functools.partial(x_kernel, start, m),
             out_shape=(shape(5, NY, m, NZ, 128), shape(5, HALO, m, NZ, 128), shape(5, HALO, m, NZ, 128)),
             compiler_params=SMALL,
+            scratch_shapes=[pltpu.VMEM((5, 144, m * NY * NZ), F32), pltpu.VMEM((5, 128, m * NY * NZ), F32)],
             cost_estimate=cost(m, 1500),
             name=f"x{start}",
         )(prims)
 
     def y_sweep(start, m, s, f, b):
         w = m * NY
+        kernel = functools.partial(y_kernel, m)
+        swapped = start > 0
         return pl.pallas_call(
-            functools.partial(y_kernel, m),
+            (lambda s, b, f, *rest: kernel(s, f, b, *rest)) if swapped else kernel,
             out_shape=(shape(5, NZ * w, 128), shape(5, HALO * w, 128), shape(5, HALO * w, 128)),
             compiler_params=SMALL,
             cost_estimate=cost(m, 1000),
             name=f"y{start}",
-        )(s, f, b)
+        )(s, *((b, f) if swapped else (f, b)))
 
     def z_sweep(start, m, t, f, b, out):
         w = m * NY

time: 33 us -> 32.8 us (level)
  Pallas kernels: 7.62 us -> 7.1 us
  starting transfers between devices: 14.1 us -> 14.5 us
    ppermute x2, starting transfers between devices: 0.01 us -> 0.62 us  [local(): lax.ppermute(b, 'row', inside)]
    pallas_call x2, Pallas kernels: 2.99 us -> 2.47 us  [x_sweep(): pl.pallas_call(functools.partial(x_kernel, start, m), out_shape=(shape(5,...]
where the time goes in v2:
time: 32.8 us; the launch traced here: 32.6 us
  starting transfers between devices  14.5 us (44%)
  waiting for transfers between devices  9.83 us (30%)
  Pallas kernels  7.1 us (22%)
  other arithmetic  1.13 us (3%)
    ppermute x2, starting transfers between devices, local(): lax.ppermute(b, 'col', inside)  7.17 us
    ppermute x2, waiting for transfers between devices, local(): lax.ppermute(f, 'row', across)  4.38 us
    ppermute x2, starting transfers between devices, local(): lax.ppermute(f, 'row', across)  3.92 us
    ppermute x2, waiting for transfers between devices, local(): lax.ppermute(f, 'col', across)  3.11 us
    ppermute x2, starting transfers between devices, local(): lax.ppermute(f, 'col', across)  2.77 us
    pallas_call x2, Pallas kernels, z_sweep(): pl.pallas_call((lambda t, b, f, *rest: kernel(t, b, f, None, *rest)) if f...  2.75 us
    pallas_call x2, Pallas kernels, x_sweep(): pl.pallas_call(functools.partial(x_kernel, start, m), out_shape=(shape(5,...  2.47 us
    ppermute x2, waiting for transfers between devices, local(): lax.ppermute(b, 'col', inside)  2.33 us
  transfers between devices with their start and end apart: 8, of which 3 were waited for; matrix products, arithmetic and copies ran while one was open for 0% of the time, Pallas kernels for 14%

profile of v2, /device:TPU:4, one launch (start us, length us, event | category | flops | bytes accessed | tf_op | source)
XLA Modules:
  0.0 32.6 jit_solution(8654256918070027046)
XLA Ops:
  0.0 1.1 %pad_maximum_fusion.q_ref = f32[5,256,128]{2,1,0:T(8,128)S(1)} fusion(f32[1,256,128]{2,1,0:T(8,128)} %bitcast.21, f32[3,256,128]{2,1,0:T(8,128)} %bitcast.20, f32[1,256,128]{2,1,0:T(8,128)} %bitcast.22), kind=kLoop, calls=%fused_computation | loop fusion | flops 327680 | bytes 1310720 | tf_op jit(solution)/shard_map/concatenate | solution.py:238
  1.1 1.2 %x0.1 = (f32[5,4,4,8,128]{4,3,2,1,0:T(8,128)S(1)}, f32[5,3,4,8,128]{4,3,2,1,0:T(8,128)S(1)}, f32[5,3,4,8,128]{4,3,2,1,0:T(8,128)S(1)}) custom-call(f32[5,256,128]{2,1,0:T(8,128)S(1)} %pad_maximum_fusion.q_ref), custom_call_target="tpu_custom_call" | custom-call | flops 24576000 | bytes 1310720 | tf_op jit(solution)/shard_map/x0/pallas_call | solution.py:241
  2.4 3.2 %collective-permute-start.4 = (f32[5,3,4,8,128]{4,3,2,1,0:T(8,128)S(1)}, f32[5,3,4,8,128]{4,3,2,1,0:T(8,128)S(1)}, u32[]{:S(2)}, u32[]{:S(2)}) collective-permute-start(f32[5,3,4,8,128]{4,3,2,1,0:T(8,128)S(1)} %get-tuple-element.24), channel_id=1, source_target_pairs={{0,240},{16,32},{32,16},{48,64},{64,48},{80,96},{96,80},{112,128},... | collective-permute-start | bytes 737288 | tf_op jit(solution)/shard_map/ppermute | solution.py:283
  5.6 0.0 collective-permute-start.5
  5.6 1.2 %x4.1 = (f32[5,4,4,8,128]{4,3,2,1,0:T(8,128)S(1)}, f32[5,3,4,8,128]{4,3,2,1,0:T(8,128)S(1)}, f32[5,3,4,8,128]{4,3,2,1,0:T(8,128)S(1)}) custom-call(f32[5,256,128]{2,1,0:T(8,128)S(1)} %pad_maximum_fusion.q_ref), custom_call_target="tpu_custom_call" | custom-call | flops 24576000 | bytes 1310720 | tf_op jit(solution)/shard_map/x4/pallas_call | solution.py:241
  6.8 0.6 %collective-permute-start = (f32[5,3,4,8,128]{4,3,2,1,0:T(8,128)S(1)}, f32[5,3,4,8,128]{4,3,2,1,0:T(8,128)S(1)}, u32[]{:S(2)}, u32[]{:S(2)}) collective-permute-start(f32[5,3,4,8,128]{4,3,2,1,0:T(8,128)S(1)} %get-tuple-element.18), channel_id=1, source_target_pairs={{0,16},{16,0},{32,48},{48,32},{64,80},{80,64},{96,112},{112,96},{1... | collective-permute-start | bytes 737288 | tf_op jit(solution)/shard_map/ppermute | solution.py:283
  7.4 0.7 %collective-permute-start.1 = (f32[5,3,4,8,128]{4,3,2,1,0:T(8,128)S(1)}, f32[5,3,4,8,128]{4,3,2,1,0:T(8,128)S(1)}, u32[]{:S(2)}, u32[]{:S(2)}) collective-permute-start(f32[5,3,4,8,128]{4,3,2,1,0:T(8,128)S(1)} %get-tuple-element.19), channel_id=1, source_target_pairs={{0,240},{16,32},{32,16},{48,64},{64,48},{80,96},{96,80},{112,128},... | collective-permute-start | bytes 737288 | tf_op jit(solution)/shard_map/ppermute | solution.py:283
  8.2 4.4 %collective-permute-done.4.f_in = f32[5,3,4,8,128]{4,3,2,1,0:T(8,128)S(1)} collective-permute-done((f32[5,3,4,8,128]{4,3,2,1,0:T(8,128)S(1)}, f32[5,3,4,8,128]{4,3,2,1,0:T(8,128)S(1)}, u32[]{:S(2)}, u32[]{:S(2)}) %collective-permute-start.4) | collective-permute-done | bytes 245792 | tf_op jit(solution)/shard_map/ppermute | solution.py:283
  12.5 0.0 collective-permute-done.5.b_in
  12.5 0.9 %y0.1 = (f32[5,128,128]{2,1,0:T(8,128)S(1)}, f32[5,48,128]{2,1,0:T(8,128)S(1)}, f32[5,48,128]{2,1,0:T(8,128)S(1)}) custom-call(f32[5,4,4,8,128]{4,3,2,1,0:T(8,128)S(1)} %get-tuple-element.23.s_ref, f32[5,3,4,8,128]{4,3,2,1,0:T(8,128)S(1)} %collective-permute-done.4.f_in, f32[5,3,4,8,128]{4,3,2,1,0:T(8,128)S(1)} %collective-permute-done.5.b_in), custom_call_target="tpu_custom_call" | custom-call | flops 16384000 | bytes 1310720 | tf_op jit(solution)/shard_map/y0/pallas_call | solution.py:254
  13.5 2.7 %collective-permute-start.6 = (f32[5,48,128]{2,1,0:T(8,128)S(1)}, f32[5,48,128]{2,1,0:T(8,128)S(1)}, u32[]{:S(2)}, u32[]{:S(2)}) collective-permute-start(f32[5,48,128]{2,1,0:T(8,128)S(1)} %get-tuple-element.27), channel_id=1, source_target_pairs={{0,1},{1,0},{2,3},{3,2},{4,5},{5,4},{6,7},{7,6},{8,9},{9,8},{10,11... | collective-permute-start | bytes 368648 | tf_op jit(solution)/shard_map/ppermute | solution.py:287
  16.1 2.3 %collective-permute-start.7 = (f32[5,48,128]{2,1,0:T(8,128)S(1)}, f32[5,48,128]{2,1,0:T(8,128)S(1)}, u32[]{:S(2)}, u32[]{:S(2)}) collective-permute-start(f32[5,48,128]{2,1,0:T(8,128)S(1)} %get-tuple-element.28), channel_id=1, source_target_pairs={{0,15},{1,2},{2,1},{3,4},{4,3},{5,6},{6,5},{7,8},{8,7},{9,10},{10,... | collective-permute-start | bytes 368648 | tf_op jit(solution)/shard_map/ppermute | solution.py:287
  18.5 0.0 collective-permute-done.b
  18.5 0.0 collective-permute-done.1.f
  18.5 0.9 %y4.1 = (f32[5,128,128]{2,1,0:T(8,128)S(1)}, f32[5,48,128]{2,1,0:T(8,128)S(1)}, f32[5,48,128]{2,1,0:T(8,128)S(1)}) custom-call(f32[5,4,4,8,128]{4,3,2,1,0:T(8,128)S(1)} %get-tuple-element.17.s, f32[5,3,4,8,128]{4,3,2,1,0:T(8,128)S(1)} %collective-permute-done.b, f32[5,3,4,8,128]{4,3,2,1,0:T(8,128)S(1)} %collective-permute-done.1.f), custom_call_target="tpu_custom_call" | custom-call | flops 16384000 | bytes 1310720 | tf_op jit(solution)/shard_map/y4/pallas_call | solution.py:254
  19.4 4.5 %collective-permute-start.2 = (f32[5,48,128]{2,1,0:T(8,128)S(1)}, f32[5,48,128]{2,1,0:T(8,128)S(1)}, u32[]{:S(2)}, u32[]{:S(2)}) collective-permute-start(f32[5,48,128]{2,1,0:T(8,128)S(1)} %get-tuple-element.21), channel_id=1, source_target_pairs={{0,1},{1,0},{2,3},{3,2},{4,5},{5,4},{6,7},{7,6},{8,9},{9,8},{10,11... | collective-permute-start | bytes 368648 | tf_op jit(solution)/shard_map/ppermute | solution.py:287
  23.9 0.5 %collective-permute-start.3 = (f32[5,48,128]{2,1,0:T(8,128)S(1)}, f32[5,48,128]{2,1,0:T(8,128)S(1)}, u32[]{:S(2)}, u32[]{:S(2)}) collective-permute-start(f32[5,48,128]{2,1,0:T(8,128)S(1)} %get-tuple-element.22), channel_id=1, source_target_pairs={{0,15},{1,2},{2,1},{3,4},{4,3},{5,6},{6,5},{7,8},{8,7},{9,10},{10,... | collective-permute-start | bytes 368648 | tf_op jit(solution)/shard_map/ppermute | solution.py:287
  24.4 0.0 collective-permute-done.6.b
  24.4 0.0 collective-permute-done.7.f
  24.4 1.4 %z0.1._ = f32[5,8,32,128]{3,2,1,0:T(8,128)} custom-call(f32[5,128,128]{2,1,0:T(8,128)S(1)} %get-tuple-element.26.t, f32[5,48,128]{2,1,0:T(8,128)S(1)} %collective-permute-done.6.b, f32[5,48,128]{2,1,0:T(8,128)S(1)} %collective-permute-done.7.f), custom_call_target="tpu_custom_call" | custom-call | flops 16384000 | bytes 1310720 | tf_op jit(solution)/shard_map/z0/pallas_call | solution.py:268
  25.8 2.3 %collective-permute-done.2.b_in = f32[5,48,128]{2,1,0:T(8,128)S(1)} collective-permute-done((f32[5,48,128]{2,1,0:T(8,128)S(1)}, f32[5,48,128]{2,1,0:T(8,128)S(1)}, u32[]{:S(2)}, u32[]{:S(2)}) %collective-permute-start.2) | collective-permute-done | bytes 122912 | tf_op jit(solution)/shard_map/ppermute | solution.py:287
  28.1 3.1 %collective-permute-done.3.f_in = f32[5,48,128]{2,1,0:T(8,128)S(1)} collective-permute-done((f32[5,48,128]{2,1,0:T(8,128)S(1)}, f32[5,48,128]{2,1,0:T(8,128)S(1)}, u32[]{:S(2)}, u32[]{:S(2)}) %collective-permute-start.3) | collective-permute-done | bytes 122912 | tf_op jit(solution)/shard_map/ppermute | solution.py:287
  31.2 1.4 %z4.1 = f32[5,8,32,128]{3,2,1,0:T(8,128)} custom-call(f32[5,128,128]{2,1,0:T(8,128)S(1)} %get-tuple-element.20.t_ref, f32[5,48,128]{2,1,0:T(8,128)S(1)} %collective-permute-done.2.b_in, f32[5,48,128]{2,1,0:T(8,128)S(1)} %collective-permute-done.3.f_in, f32[5,8,32,128]{3,2,1,0:T(8,128)} %z0.1._), custom_call_target="tpu_custom_call", output_to_operand_aliasing={{}: (3, {})} | custom-call | flops 16384000 | bytes 1310720 | tf_op jit(solution)/shard_map/z4/pallas_call | solution.py:268
Async XLA Ops:
  2.4 10.2 %collective-permute-start.4 = (f32[5,3,4,8,128]{4,3,2,1,0:T(8,128)S(1)}, f32[5,3,4,8,128]{4,3,2,1,0:T(8,128)S(1)}, u32[]{:S(2)}, u32[]{:S(2)}) collective-permute-start(f32[5,3,4,8,128]{4,3,2,1,0:T(8,128)S(1)} %get-tuple-element.24), channel_id=1, source_target_pairs={{0,240},{16,32},{32,16},{48,64},{64,48},{80,96},{96,80},{112,128},... | collective-permute-start | bytes 737288 | tf_op jit(solution)/shard_map/ppermute | solution.py:283
  5.6 7.0 %collective-permute-start.5 = (f32[5,3,4,8,128]{4,3,2,1,0:T(8,128)S(1)}, f32[5,3,4,8,128]{4,3,2,1,0:T(8,128)S(1)}, u32[]{:S(2)}, u32[]{:S(2)}) collective-permute-start(f32[5,3,4,8,128]{4,3,2,1,0:T(8,128)S(1)} %get-tuple-element.25), channel_id=1, source_target_pairs={{0,16},{16,0},{32,48},{48,32},{64,80},{80,64},{96,112},{112,96},{1... | collective-permute-start | bytes 737288 | tf_op jit(solution)/shard_map/ppermute | solution.py:283
  6.8 11.6 %collective-permute-start = (f32[5,3,4,8,128]{4,3,2,1,0:T(8,128)S(1)}, f32[5,3,4,8,128]{4,3,2,1,0:T(8,128)S(1)}, u32[]{:S(2)}, u32[]{:S(2)}) collective-permute-start(f32[5,3,4,8,128]{4,3,2,1,0:T(8,128)S(1)} %get-tuple-element.18), channel_id=1, source_target_pairs={{0,16},{16,0},{32,48},{48,32},{64,80},{80,64},{96,112},{112,96},{1... | collective-permute-start | bytes 737288 | tf_op jit(solution)/shard_map/ppermute | solution.py:283
  7.4 11.0 %collective-permute-start.1 = (f32[5,3,4,8,128]{4,3,2,1,0:T(8,128)S(1)}, f32[5,3,4,8,128]{4,3,2,1,0:T(8,128)S(1)}, u32[]{:S(2)}, u32[]{:S(2)}) collective-permute-start(f32[5,3,4,8,128]{4,3,2,1,0:T(8,128)S(1)} %get-tuple-element.19), channel_id=1, source_target_pairs={{0,240},{16,32},{32,16},{48,64},{64,48},{80,96},{96,80},{112,128},... | collective-permute-start | bytes 737288 | tf_op jit(solution)/shard_map/ppermute | solution.py:283
  13.5 10.9 %collective-permute-start.6 = (f32[5,48,128]{2,1,0:T(8,128)S(1)}, f32[5,48,128]{2,1,0:T(8,128)S(1)}, u32[]{:S(2)}, u32[]{:S(2)}) collective-permute-start(f32[5,48,128]{2,1,0:T(8,128)S(1)} %get-tuple-element.27), channel_id=1, source_target_pairs={{0,1},{1,0},{2,3},{3,2},{4,5},{5,4},{6,7},{7,6},{8,9},{9,8},{10,11... | collective-permute-start | bytes 368648 | tf_op jit(solution)/shard_map/ppermute | solution.py:287
  16.1 8.2 %collective-permute-start.7 = (f32[5,48,128]{2,1,0:T(8,128)S(1)}, f32[5,48,128]{2,1,0:T(8,128)S(1)}, u32[]{:S(2)}, u32[]{:S(2)}) collective-permute-start(f32[5,48,128]{2,1,0:T(8,128)S(1)} %get-tuple-element.28), channel_id=1, source_target_pairs={{0,15},{1,2},{2,1},{3,4},{4,3},{5,6},{6,5},{7,8},{8,7},{9,10},{10,... | collective-permute-start | bytes 368648 | tf_op jit(solution)/shard_map/ppermute | solution.py:287
  19.4 8.7 %collective-permute-start.2 = (f32[5,48,128]{2,1,0:T(8,128)S(1)}, f32[5,48,128]{2,1,0:T(8,128)S(1)}, u32[]{:S(2)}, u32[]{:S(2)}) collective-permute-start(f32[5,48,128]{2,1,0:T(8,128)S(1)} %get-tuple-element.21), channel_id=1, source_target_pairs={{0,1},{1,0},{2,3},{3,2},{4,5},{5,4},{6,7},{7,6},{8,9},{9,8},{10,11... | collective-permute-start | bytes 368648 | tf_op jit(solution)/shard_map/ppermute | solution.py:287
  23.9 7.3 %collective-permute-start.3 = (f32[5,48,128]{2,1,0:T(8,128)S(1)}, f32[5,48,128]{2,1,0:T(8,128)S(1)}, u32[]{:S(2)}, u32[]{:S(2)}) collective-permute-start(f32[5,48,128]{2,1,0:T(8,128)S(1)} %get-tuple-element.22), channel_id=1, source_target_pairs={{0,15},{1,2},{2,1},{3,4},{4,3},{5,6},{6,5},{7,8},{8,7},{9,10},{10,... | collective-permute-start | bytes 368648 | tf_op jit(solution)/shard_map/ppermute | solution.py:287

commit v3 on v2

--- a/solution.py
+++ b/solution.py
@@ -204,6 +204,59 @@
         copy.wait()
 
 
+def z_inner(per, t_ref, q_ref, mid_ref):
+    for r in range(0, per * NY, 8):
+        at = slice(r, r + 8)
+        own = [[t_ref[c, z * per * NY + r : z * per * NY + r + 8] for c in range(5)] for z in range(NZ)]
+        q = [primitives(u, (3, 1, 2)) for u in own]
+        face = {k: [face_values(*(q[k + i][c] for i in (-1, 0, 1, 2))) for c in range(5)] for k in range(1, 6)}
+        edge = {k: [cell_edges(q[k][c], face[k - 1][c], face[k][c]) for c in range(5)] for k in range(2, 6)}
+        flux = [riemann([e[1] for e in edge[k]], [e[0] for e in edge[k + 1]]) for k in (2, 3, 4)]
+        kept = [face[1], face[5], [e[0] for e in edge[2]], [e[1] for e in edge[5]]] + flux
+        for c in range(5):
+            for z in range(NZ):
+                q_ref[c, z, at] = q[z][c]
+            for i, v in enumerate(kept):
+                mid_ref[c, i, at] = v[c]
+
+
+def z_outer(start, per, t_ref, q_ref, mid_ref, b_in, f_in, _, o_hbm, o_ref, sems):
+    width = per * NY
+    odd = lax.rem(lax.axis_index("col"), 2) == 1
+    copies = []
+    for i, r in enumerate(range(0, width, 8)):
+        at = slice(r, r + 8)
+
+        def halo(even_ref, odd_ref, z):
+            rows_at = slice(z * width + r, z * width + r + 8)
+            picked = [jnp.where(odd, odd_ref[c, rows_at], even_ref[c, rows_at]) for c in range(5)]
+            return primitives(picked, (3, 1, 2))
+
+        q = {z: [q_ref[c, z, at] for c in range(5)] for z in range(NZ)}
+        q.update({z - HALO: halo(f_in, b_in, z) for z in range(HALO)})
+        q.update({z + NZ: halo(b_in, f_in, z) for z in range(HALO)})
+        kept = [[mid_ref[c, j, at] for c in range(5)] for j in range(7)]
+        face = {1: kept[0], 5: kept[1]}
+        for k in (-2, -1, 0, 6, 7, 8):
+            face[k] = [face_values(*(q[k + j][c] for j in (-1, 0, 1, 2))) for c in range(5)]
+        low, high = {2: kept[2]}, {5: kept[3]}
+        for k in (-1, 0, 1, 6, 7, 8):
+            both = [cell_edges(q[k][c], face[k - 1][c], face[k][c]) for c in range(5)]
+            low[k], high[k] = [e[0] for e in both], [e[1] for e in both]
+        flux = {2: kept[4], 3: kept[5], 4: kept[6]}
+        for k in (-1, 0, 1, 5, 6, 7):
+            flux[k] = riemann(high[k], low[k + 1])
+        for z in range(NZ):
+            for k, c in enumerate((0, 3, 1, 2, 4)):
+                old = t_ref[c, z * width + r : z * width + r + 8]
+                o_ref[c, z, at] = old - DTDX * (flux[z][k] - flux[z - 1][k])
+        rows_out = slice(start * NY + r, start * NY + r + 8)
+        copies.append(pltpu.make_async_copy(o_ref.at[:, :, at], o_hbm.at[:, :, rows_out], sems.at[i]))
+        copies[-1].start()
+    for copy in copies:
+        copy.wait()
+
+
 def rows(a):
     lead = a.shape[:-3]
     a = jnp.swapaxes(a.reshape(*lead, NZ, NY, TILES, 128), -2, -3)
@@ -277,6 +330,29 @@
             name=f"z{start}",
         )(t, b, f, *([] if first else [out]))
 
+    def z_split(start, m, t, f, b, out):
+        w = m * NY
+        near = pl.BlockSpec(memory_space=pltpu.VMEM)
+        far = pl.BlockSpec(memory_space=pl.ANY)
+        q, mid = pl.pallas_call(
+            functools.partial(z_inner, m),
+            out_shape=(shape(5, NZ, w, 128), shape(5, 7, w, 128)),
+            compiler_params=SMALL,
+            cost_estimate=cost(m, 500),
+            name=f"inner{start}",
+        )(t)
+        return pl.pallas_call(
+            functools.partial(z_outer, start, m),
+            in_specs=[near] * 5 + [far],
+            out_specs=far,
+            out_shape=shape(5, NZ, TILES * NY, 128),
+            scratch_shapes=[pltpu.VMEM((5, NZ, w, 128), F32), pltpu.SemaphoreType.DMA((w // 8,))],
+            input_output_aliases={5: 0},
+            compiler_params=SMALL,
+            cost_estimate=cost(m, 700),
+            name=f"z{start}",
+        )(t, q, mid, b, f, out)
+
     y_in = []
     for start, m in chunks:
         s, f, b = x_sweep(start, m)
@@ -287,7 +363,7 @@
         z_in.append((t, lax.ppermute(b, "col", inside), lax.ppermute(f, "col", across)))
     out = None
     for (start, m), (t, b, f) in zip(chunks, z_in):
-        out = z_sweep(start, m, t, f, b, out)
+        out = (z_split if start else z_sweep)(start, m, t, f, b, out)
     return unrows(out)
 
 

time: 32.8 us -> 32.6 us (level)
    pallas_call x0 -> x2, Pallas kernels: none -> 1.46 us  [the longest x1 1.17 us: z_split(): pl.pallas_call(functools.partial(z_outer, start, m), in_specs=[near] * 5...]
    pallas_call x2 -> x1, Pallas kernels: 2.75 us -> 1.38 us  [z_sweep(): pl.pallas_call((lambda t, b, f, *rest: kernel(t, b, f, None, *rest)) if f...]
  transfers between devices with their start and end apart: 8 -> 8, of which waited for: 3 -> 3; matrix products, arithmetic and copies ran while one was open for 0% -> 0% of each run, Pallas kernels for 14% -> 15%
where the time goes in v3:
time: 32.6 us; the launch traced here: 32.4 us
  starting transfers between devices  14.5 us (44%)
  waiting for transfers between devices  9.52 us (29%)
  Pallas kernels  7.19 us (22%)
  other arithmetic  1.13 us (3%)
    ppermute x2, starting transfers between devices, local(): lax.ppermute(b, 'col', inside)  7.17 us
    ppermute x2, waiting for transfers between devices, local(): lax.ppermute(f, 'row', across)  4.38 us
    ppermute x2, starting transfers between devices, local(): lax.ppermute(f, 'row', across)  3.92 us
    ppermute x2, waiting for transfers between devices, local(): lax.ppermute(f, 'col', across)  3.11 us
    ppermute x2, starting transfers between devices, local(): lax.ppermute(f, 'col', across)  2.77 us
    pallas_call x2, Pallas kernels, x_sweep(): pl.pallas_call(functools.partial(x_kernel, start, m), out_shape=(shape(5,...  2.48 us
    ppermute x2, waiting for transfers between devices, local(): lax.ppermute(b, 'col', inside)  2.02 us
    pallas_call x2, Pallas kernels, y_sweep(): pl.pallas_call((lambda s, b, f, *rest: kernel(s, f, b, *rest)) if swapped...  1.87 us
  transfers between devices with their start and end apart: 8, of which 3 were waited for; matrix products, arithmetic and copies ran while one was open for 0% of the time, Pallas kernels for 15%

profile of v3, /device:TPU:4, one launch (start us, length us, event | category | flops | bytes accessed | tf_op | source)
XLA Modules:
  0.0 32.4 jit_solution(9221571279679896881)
XLA Ops:
  0.0 1.1 %pad_maximum_fusion.q_ref = f32[5,256,128]{2,1,0:T(8,128)S(1)} fusion(f32[1,256,128]{2,1,0:T(8,128)} %bitcast.21, f32[3,256,128]{2,1,0:T(8,128)} %bitcast.20, f32[1,256,128]{2,1,0:T(8,128)} %bitcast.22), kind=kLoop, calls=%fused_computation | loop fusion | flops 327680 | bytes 1310720 | tf_op jit(solution)/shard_map/concatenate | solution.py:291
  1.1 1.2 %x0.1 = (f32[5,4,4,8,128]{4,3,2,1,0:T(8,128)S(1)}, f32[5,3,4,8,128]{4,3,2,1,0:T(8,128)S(1)}, f32[5,3,4,8,128]{4,3,2,1,0:T(8,128)S(1)}) custom-call(f32[5,256,128]{2,1,0:T(8,128)S(1)} %pad_maximum_fusion.q_ref), custom_call_target="tpu_custom_call" | custom-call | flops 24576000 | bytes 1310720 | tf_op jit(solution)/shard_map/x0/pallas_call | solution.py:294
  2.4 3.2 %collective-permute-start.4 = (f32[5,3,4,8,128]{4,3,2,1,0:T(8,128)S(1)}, f32[5,3,4,8,128]{4,3,2,1,0:T(8,128)S(1)}, u32[]{:S(2)}, u32[]{:S(2)}) collective-permute-start(f32[5,3,4,8,128]{4,3,2,1,0:T(8,128)S(1)} %get-tuple-element.28), channel_id=1, source_target_pairs={{0,240},{16,32},{32,16},{48,64},{64,48},{80,96},{96,80},{112,128},... | collective-permute-start | bytes 737288 | tf_op jit(solution)/shard_map/ppermute | solution.py:359
  5.6 0.0 collective-permute-start.5
  5.6 1.2 %x4.1 = (f32[5,4,4,8,128]{4,3,2,1,0:T(8,128)S(1)}, f32[5,3,4,8,128]{4,3,2,1,0:T(8,128)S(1)}, f32[5,3,4,8,128]{4,3,2,1,0:T(8,128)S(1)}) custom-call(f32[5,256,128]{2,1,0:T(8,128)S(1)} %pad_maximum_fusion.q_ref), custom_call_target="tpu_custom_call" | custom-call | flops 24576000 | bytes 1310720 | tf_op jit(solution)/shard_map/x4/pallas_call | solution.py:294
  6.8 0.6 %collective-permute-start = (f32[5,3,4,8,128]{4,3,2,1,0:T(8,128)S(1)}, f32[5,3,4,8,128]{4,3,2,1,0:T(8,128)S(1)}, u32[]{:S(2)}, u32[]{:S(2)}) collective-permute-start(f32[5,3,4,8,128]{4,3,2,1,0:T(8,128)S(1)} %get-tuple-element.20), channel_id=1, source_target_pairs={{0,16},{16,0},{32,48},{48,32},{64,80},{80,64},{96,112},{112,96},{1... | collective-permute-start | bytes 737288 | tf_op jit(solution)/shard_map/ppermute | solution.py:359
  7.4 0.7 %collective-permute-start.1 = (f32[5,3,4,8,128]{4,3,2,1,0:T(8,128)S(1)}, f32[5,3,4,8,128]{4,3,2,1,0:T(8,128)S(1)}, u32[]{:S(2)}, u32[]{:S(2)}) collective-permute-start(f32[5,3,4,8,128]{4,3,2,1,0:T(8,128)S(1)} %get-tuple-element.21), channel_id=1, source_target_pairs={{0,240},{16,32},{32,16},{48,64},{64,48},{80,96},{96,80},{112,128},... | collective-permute-start | bytes 737288 | tf_op jit(solution)/shard_map/ppermute | solution.py:359
  8.2 4.4 %collective-permute-done.4.f_in = f32[5,3,4,8,128]{4,3,2,1,0:T(8,128)S(1)} collective-permute-done((f32[5,3,4,8,128]{4,3,2,1,0:T(8,128)S(1)}, f32[5,3,4,8,128]{4,3,2,1,0:T(8,128)S(1)}, u32[]{:S(2)}, u32[]{:S(2)}) %collective-permute-start.4) | collective-permute-done | bytes 245792 | tf_op jit(solution)/shard_map/ppermute | solution.py:359
  12.5 0.0 collective-permute-done.5.b_in
  12.5 0.9 %y0.1 = (f32[5,128,128]{2,1,0:T(8,128)S(1)}, f32[5,48,128]{2,1,0:T(8,128)S(1)}, f32[5,48,128]{2,1,0:T(8,128)S(1)}) custom-call(f32[5,4,4,8,128]{4,3,2,1,0:T(8,128)S(1)} %get-tuple-element.27.s_ref, f32[5,3,4,8,128]{4,3,2,1,0:T(8,128)S(1)} %collective-permute-done.4.f_in, f32[5,3,4,8,128]{4,3,2,1,0:T(8,128)S(1)} %collective-permute-done.5.b_in), custom_call_target="tpu_custom_call" | custom-call | flops 16384000 | bytes 1310720 | tf_op jit(solution)/shard_map/y0/pallas_call | solution.py:307
  13.5 2.7 %collective-permute-start.6 = (f32[5,48,128]{2,1,0:T(8,128)S(1)}, f32[5,48,128]{2,1,0:T(8,128)S(1)}, u32[]{:S(2)}, u32[]{:S(2)}) collective-permute-start(f32[5,48,128]{2,1,0:T(8,128)S(1)} %get-tuple-element.31), channel_id=1, source_target_pairs={{0,1},{1,0},{2,3},{3,2},{4,5},{5,4},{6,7},{7,6},{8,9},{9,8},{10,11... | collective-permute-start | bytes 368648 | tf_op jit(solution)/shard_map/ppermute | solution.py:363
  16.1 2.3 %collective-permute-start.7 = (f32[5,48,128]{2,1,0:T(8,128)S(1)}, f32[5,48,128]{2,1,0:T(8,128)S(1)}, u32[]{:S(2)}, u32[]{:S(2)}) collective-permute-start(f32[5,48,128]{2,1,0:T(8,128)S(1)} %get-tuple-element.32), channel_id=1, source_target_pairs={{0,15},{1,2},{2,1},{3,4},{4,3},{5,6},{6,5},{7,8},{8,7},{9,10},{10,... | collective-permute-start | bytes 368648 | tf_op jit(solution)/shard_map/ppermute | solution.py:363
  18.5 0.0 collective-permute-done.b
  18.5 0.0 collective-permute-done.1.f
  18.5 0.9 %y4.1 = (f32[5,128,128]{2,1,0:T(8,128)S(1)}, f32[5,48,128]{2,1,0:T(8,128)S(1)}, f32[5,48,128]{2,1,0:T(8,128)S(1)}) custom-call(f32[5,4,4,8,128]{4,3,2,1,0:T(8,128)S(1)} %get-tuple-element.19.s, f32[5,3,4,8,128]{4,3,2,1,0:T(8,128)S(1)} %collective-permute-done.b, f32[5,3,4,8,128]{4,3,2,1,0:T(8,128)S(1)} %collective-permute-done.1.f), custom_call_target="tpu_custom_call" | custom-call | flops 16384000 | bytes 1310720 | tf_op jit(solution)/shard_map/y4/pallas_call | solution.py:307
  19.4 4.5 %collective-permute-start.2 = (f32[5,48,128]{2,1,0:T(8,128)S(1)}, f32[5,48,128]{2,1,0:T(8,128)S(1)}, u32[]{:S(2)}, u32[]{:S(2)}) collective-permute-start(f32[5,48,128]{2,1,0:T(8,128)S(1)} %get-tuple-element.25), channel_id=1, source_target_pairs={{0,1},{1,0},{2,3},{3,2},{4,5},{5,4},{6,7},{7,6},{8,9},{9,8},{10,11... | collective-permute-start | bytes 368648 | tf_op jit(solution)/shard_map/ppermute | solution.py:363
  23.9 0.5 %collective-permute-start.3 = (f32[5,48,128]{2,1,0:T(8,128)S(1)}, f32[5,48,128]{2,1,0:T(8,128)S(1)}, u32[]{:S(2)}, u32[]{:S(2)}) collective-permute-start(f32[5,48,128]{2,1,0:T(8,128)S(1)} %get-tuple-element.26), channel_id=1, source_target_pairs={{0,15},{1,2},{2,1},{3,4},{4,3},{5,6},{6,5},{7,8},{8,7},{9,10},{10,... | collective-permute-start | bytes 368648 | tf_op jit(solution)/shard_map/ppermute | solution.py:363
  24.4 0.3 inner4.1
  24.7 0.0 collective-permute-done.6.b
  24.7 0.0 collective-permute-done.7.f
  24.7 1.4 %z0.1._ = f32[5,8,32,128]{3,2,1,0:T(8,128)} custom-call(f32[5,128,128]{2,1,0:T(8,128)S(1)} %get-tuple-element.30.t, f32[5,48,128]{2,1,0:T(8,128)S(1)} %collective-permute-done.6.b, f32[5,48,128]{2,1,0:T(8,128)S(1)} %collective-permute-done.7.f), custom_call_target="tpu_custom_call" | custom-call | flops 16384000 | bytes 1310720 | tf_op jit(solution)/shard_map/z0/pallas_call | solution.py:321
  26.1 2.0 %collective-permute-done.2.b_in = f32[5,48,128]{2,1,0:T(8,128)S(1)} collective-permute-done((f32[5,48,128]{2,1,0:T(8,128)S(1)}, f32[5,48,128]{2,1,0:T(8,128)S(1)}, u32[]{:S(2)}, u32[]{:S(2)}) %collective-permute-start.2) | collective-permute-done | bytes 122912 | tf_op jit(solution)/shard_map/ppermute | solution.py:363
  28.1 3.1 %collective-permute-done.3.f_in = f32[5,48,128]{2,1,0:T(8,128)S(1)} collective-permute-done((f32[5,48,128]{2,1,0:T(8,128)S(1)}, f32[5,48,128]{2,1,0:T(8,128)S(1)}, u32[]{:S(2)}, u32[]{:S(2)}) %collective-permute-start.3) | collective-permute-done | bytes 122912 | tf_op jit(solution)/shard_map/ppermute | solution.py:363
  31.2 1.2 %z4.1 = f32[5,8,32,128]{3,2,1,0:T(8,128)} custom-call(f32[5,128,128]{2,1,0:T(8,128)S(1)} %get-tuple-element.22.t_ref, f32[5,8,16,128]{3,2,1,0:T(8,128)S(1)} %get-tuple-element.23.q_ref, f32[5,7,16,128]{3,2,1,0:T(8,128)S(1)} %get-tuple-element.24.mid_ref, f32[5,48,128]{2,1,0:T(8,128)S(1)} %collective-permute-done.2.b_in, ...), custom_call_target="tpu_custom_call", output_to_operand_aliasing={{}: (5, {})} | custom-call | flops 11468800 | bytes 1310720 | tf_op jit(solution)/shard_map/z4/pallas_call | solution.py:344
Async XLA Ops:
  2.4 10.2 %collective-permute-start.4 = (f32[5,3,4,8,128]{4,3,2,1,0:T(8,128)S(1)}, f32[5,3,4,8,128]{4,3,2,1,0:T(8,128)S(1)}, u32[]{:S(2)}, u32[]{:S(2)}) collective-permute-start(f32[5,3,4,8,128]{4,3,2,1,0:T(8,128)S(1)} %get-tuple-element.28), channel_id=1, source_target_pairs={{0,240},{16,32},{32,16},{48,64},{64,48},{80,96},{96,80},{112,128},... | collective-permute-start | bytes 737288 | tf_op jit(solution)/shard_map/ppermute | solution.py:359
  5.6 7.0 %collective-permute-start.5 = (f32[5,3,4,8,128]{4,3,2,1,0:T(8,128)S(1)}, f32[5,3,4,8,128]{4,3,2,1,0:T(8,128)S(1)}, u32[]{:S(2)}, u32[]{:S(2)}) collective-permute-start(f32[5,3,4,8,128]{4,3,2,1,0:T(8,128)S(1)} %get-tuple-element.29), channel_id=1, source_target_pairs={{0,16},{16,0},{32,48},{48,32},{64,80},{80,64},{96,112},{112,96},{1... | collective-permute-start | bytes 737288 | tf_op jit(solution)/shard_map/ppermute | solution.py:359
  6.8 11.6 %collective-permute-start = (f32[5,3,4,8,128]{4,3,2,1,0:T(8,128)S(1)}, f32[5,3,4,8,128]{4,3,2,1,0:T(8,128)S(1)}, u32[]{:S(2)}, u32[]{:S(2)}) collective-permute-start(f32[5,3,4,8,128]{4,3,2,1,0:T(8,128)S(1)} %get-tuple-element.20), channel_id=1, source_target_pairs={{0,16},{16,0},{32,48},{48,32},{64,80},{80,64},{96,112},{112,96},{1... | collective-permute-start | bytes 737288 | tf_op jit(solution)/shard_map/ppermute | solution.py:359
  7.4 11.0 %collective-permute-start.1 = (f32[5,3,4,8,128]{4,3,2,1,0:T(8,128)S(1)}, f32[5,3,4,8,128]{4,3,2,1,0:T(8,128)S(1)}, u32[]{:S(2)}, u32[]{:S(2)}) collective-permute-start(f32[5,3,4,8,128]{4,3,2,1,0:T(8,128)S(1)} %get-tuple-element.21), channel_id=1, source_target_pairs={{0,240},{16,32},{32,16},{48,64},{64,48},{80,96},{96,80},{112,128},... | collective-permute-start | bytes 737288 | tf_op jit(solution)/shard_map/ppermute | solution.py:359
  13.5 11.2 %collective-permute-start.6 = (f32[5,48,128]{2,1,0:T(8,128)S(1)}, f32[5,48,128]{2,1,0:T(8,128)S(1)}, u32[]{:S(2)}, u32[]{:S(2)}) collective-permute-start(f32[5,48,128]{2,1,0:T(8,128)S(1)} %get-tuple-element.31), channel_id=1, source_target_pairs={{0,1},{1,0},{2,3},{3,2},{4,5},{5,4},{6,7},{7,6},{8,9},{9,8},{10,11... | collective-permute-start | bytes 368648 | tf_op jit(solution)/shard_map/ppermute | solution.py:363
  16.1 8.5 %collective-permute-start.7 = (f32[5,48,128]{2,1,0:T(8,128)S(1)}, f32[5,48,128]{2,1,0:T(8,128)S(1)}, u32[]{:S(2)}, u32[]{:S(2)}) collective-permute-start(f32[5,48,128]{2,1,0:T(8,128)S(1)} %get-tuple-element.32), channel_id=1, source_target_pairs={{0,15},{1,2},{2,1},{3,4},{4,3},{5,6},{6,5},{7,8},{8,7},{9,10},{10,... | collective-permute-start | bytes 368648 | tf_op jit(solution)/shard_map/ppermute | solution.py:363
  19.4 8.7 %collective-permute-start.2 = (f32[5,48,128]{2,1,0:T(8,128)S(1)}, f32[5,48,128]{2,1,0:T(8,128)S(1)}, u32[]{:S(2)}, u32[]{:S(2)}) collective-permute-start(f32[5,48,128]{2,1,0:T(8,128)S(1)} %get-tuple-element.25), channel_id=1, source_target_pairs={{0,1},{1,0},{2,3},{3,2},{4,5},{5,4},{6,7},{7,6},{8,9},{9,8},{10,11... | collective-permute-start | bytes 368648 | tf_op jit(solution)/shard_map/ppermute | solution.py:363
  23.9 7.3 %collective-permute-start.3 = (f32[5,48,128]{2,1,0:T(8,128)S(1)}, f32[5,48,128]{2,1,0:T(8,128)S(1)}, u32[]{:S(2)}, u32[]{:S(2)}) collective-permute-start(f32[5,48,128]{2,1,0:T(8,128)S(1)} %get-tuple-element.26), channel_id=1, source_target_pairs={{0,15},{1,2},{2,1},{3,4},{4,3},{5,6},{6,5},{7,8},{8,7},{9,10},{10,... | collective-permute-start | bytes 368648 | tf_op jit(solution)/shard_map/ppermute | solution.py:363

commit v4 on v3

--- a/solution.py
+++ b/solution.py
@@ -171,39 +171,6 @@
         b_ref[c] = t_ref[c, pl.ds(pl.multiple_of((1 - odd) * (NZ - HALO) * width, 8), HALO * width)]
 
 
-def z_kernel(start, per, t_ref, b_in, f_in, _, o_hbm, o_ref, sems):
-    width = per * NY
-    odd = lax.rem(lax.axis_index("col"), 2) == 1
-
-    def halo(even_ref, odd_ref, c, z, r):
-        at = slice(z * width + r, z * width + r + 8)
-        return jnp.where(odd, odd_ref[c, at], even_ref[c, at])
-
-    copies = []
-    for i, r in enumerate(range(0, width, 8)):
-        full = [
-            jnp.stack(
-                [halo(f_in, b_in, c, z, r) for z in range(HALO)]
-                + [t_ref[c, z * width + r : z * width + r + 8] for z in range(NZ)]
-                + [halo(b_in, f_in, c, z, r) for z in range(HALO)]
-            )
-            for c in range(5)
-        ]
-        change = line_change(primitives(full, (3, 1, 2)), NZ)
-        for c, k in enumerate((0, 2, 3, 1, 4)):
-            new = full[c][HALO : HALO + NZ] - change[k]
-            for z in range(NZ):
-                o_ref[c, z, r : r + 8] = new[z]
-        copies.append(
-            pltpu.make_async_copy(
-                o_ref.at[:, :, r : r + 8], o_hbm.at[:, :, start * NY + r : start * NY + r + 8], sems.at[i]
-            )
-        )
-        copies[-1].start()
-    for copy in copies:
-        copy.wait()
-
-
 def z_inner(per, t_ref, q_ref, mid_ref):
     for r in range(0, per * NY, 8):
         at = slice(r, r + 8)
@@ -312,24 +279,6 @@
             name=f"y{start}",
         )(s, *((b, f) if swapped else (f, b)))
 
-    def z_sweep(start, m, t, f, b, out):
-        w = m * NY
-        first = out is None
-        near = pl.BlockSpec(memory_space=pltpu.VMEM)
-        far = pl.BlockSpec(memory_space=pl.ANY)
-        kernel = functools.partial(z_kernel, start, m)
-        return pl.pallas_call(
-            (lambda t, b, f, *rest: kernel(t, b, f, None, *rest)) if first else kernel,
-            in_specs=[near] * 3 + [far] * (not first),
-            out_specs=far,
-            out_shape=shape(5, NZ, TILES * NY, 128),
-            scratch_shapes=[pltpu.VMEM((5, NZ, w, 128), F32), pltpu.SemaphoreType.DMA((w // 8,))],
-            input_output_aliases={} if first else {3: 0},
-            compiler_params=SMALL,
-            cost_estimate=cost(m, 1000),
-            name=f"z{start}",
-        )(t, b, f, *([] if first else [out]))
-
     def z_split(start, m, t, f, b, out):
         w = m * NY
         near = pl.BlockSpec(memory_space=pltpu.VMEM)
@@ -341,17 +290,19 @@
             cost_estimate=cost(m, 500),
             name=f"inner{start}",
         )(t)
+        first = out is None
+        kernel = functools.partial(z_outer, start, m)
         return pl.pallas_call(
-            functools.partial(z_outer, start, m),
-            in_specs=[near] * 5 + [far],
+            (lambda t, q, mid, b, f, *rest: kernel(t, q, mid, b, f, None, *rest)) if first else kernel,
+            in_specs=[near] * 5 + [far] * (not first),
             out_specs=far,
             out_shape=shape(5, NZ, TILES * NY, 128),
             scratch_shapes=[pltpu.VMEM((5, NZ, w, 128), F32), pltpu.SemaphoreType.DMA((w // 8,))],
-            input_output_aliases={5: 0},
+            input_output_aliases={} if first else {5: 0},
             compiler_params=SMALL,
             cost_estimate=cost(m, 700),
             name=f"z{start}",
-        )(t, q, mid, b, f, out)
+        )(t, q, mid, b, f, *([] if first else [out]))
 
     y_in = []
     for start, m in chunks:
@@ -363,7 +314,7 @@
         z_in.append((t, lax.ppermute(b, "col", inside), lax.ppermute(f, "col", across)))
     out = None
     for (start, m), (t, b, f) in zip(chunks, z_in):
-        out = (z_split if start else z_sweep)(start, m, t, f, b, out)
+        out = z_split(start, m, t, f, b, out)
     return unrows(out)
 
 

time: 32.6 us -> 32.6 us (level)
  no operation moved by 1% of the time
where the time goes in v4:
time: 32.6 us; the launch traced here: 32.4 us
  starting transfers between devices  14.5 us (44%)
  waiting for transfers between devices  9.43 us (29%)
  Pallas kernels  7.27 us (22%)
  other arithmetic  1.13 us (3%)
    ppermute x2, starting transfers between devices, local(): lax.ppermute(b, 'col', inside)  7.17 us
    ppermute x2, waiting for transfers between devices, local(): lax.ppermute(f, 'row', across)  4.38 us
    ppermute x2, starting transfers between devices, local(): lax.ppermute(f, 'row', across)  3.92 us
    ppermute x2, waiting for transfers between devices, local(): lax.ppermute(f, 'col', across)  3.11 us
    ppermute x2, starting transfers between devices, local(): lax.ppermute(f, 'col', across)  2.77 us
    pallas_call x2, Pallas kernels, x_sweep(): pl.pallas_call(functools.partial(x_kernel, start, m), out_shape=(shape(5,...  2.48 us
    pallas_call x2, Pallas kernels, z_split(): pl.pallas_call((lambda t, q, mid, b, f, *rest: kernel(t, q, mid, b, f, No...  2.35 us
    ppermute x2, waiting for transfers between devices, local(): lax.ppermute(b, 'col', inside)  1.94 us
  transfers between devices with their start and end apart: 8, of which 3 were waited for; matrix products, arithmetic and copies ran while one was open for 0% of the time, Pallas kernels for 15%

profile of v4, /device:TPU:4, one launch (start us, length us, event | category | flops | bytes accessed | tf_op | source)
XLA Modules:
  0.0 32.4 jit_solution(12674454941839581361)
XLA Ops:
  0.0 1.1 %pad_maximum_fusion.q_ref = f32[5,256,128]{2,1,0:T(8,128)S(1)} fusion(f32[1,256,128]{2,1,0:T(8,128)} %bitcast.21, f32[3,256,128]{2,1,0:T(8,128)} %bitcast.20, f32[1,256,128]{2,1,0:T(8,128)} %bitcast.22), kind=kLoop, calls=%fused_computation | loop fusion | flops 327680 | bytes 1310720 | tf_op jit(solution)/shard_map/concatenate | solution.py:258
  1.1 1.2 %x0.1 = (f32[5,4,4,8,128]{4,3,2,1,0:T(8,128)S(1)}, f32[5,3,4,8,128]{4,3,2,1,0:T(8,128)S(1)}, f32[5,3,4,8,128]{4,3,2,1,0:T(8,128)S(1)}) custom-call(f32[5,256,128]{2,1,0:T(8,128)S(1)} %pad_maximum_fusion.q_ref), custom_call_target="tpu_custom_call" | custom-call | flops 24576000 | bytes 1310720 | tf_op jit(solution)/shard_map/x0/pallas_call | solution.py:261
  2.4 3.2 %collective-permute-start.4 = (f32[5,3,4,8,128]{4,3,2,1,0:T(8,128)S(1)}, f32[5,3,4,8,128]{4,3,2,1,0:T(8,128)S(1)}, u32[]{:S(2)}, u32[]{:S(2)}) collective-permute-start(f32[5,3,4,8,128]{4,3,2,1,0:T(8,128)S(1)} %get-tuple-element.30), channel_id=1, source_target_pairs={{0,240},{16,32},{32,16},{48,64},{64,48},{80,96},{96,80},{112,128},... | collective-permute-start | bytes 737288 | tf_op jit(solution)/shard_map/ppermute | solution.py:310
  5.6 0.0 collective-permute-start.5
  5.6 1.2 %x4.1 = (f32[5,4,4,8,128]{4,3,2,1,0:T(8,128)S(1)}, f32[5,3,4,8,128]{4,3,2,1,0:T(8,128)S(1)}, f32[5,3,4,8,128]{4,3,2,1,0:T(8,128)S(1)}) custom-call(f32[5,256,128]{2,1,0:T(8,128)S(1)} %pad_maximum_fusion.q_ref), custom_call_target="tpu_custom_call" | custom-call | flops 24576000 | bytes 1310720 | tf_op jit(solution)/shard_map/x4/pallas_call | solution.py:261
  6.8 0.6 %collective-permute-start = (f32[5,3,4,8,128]{4,3,2,1,0:T(8,128)S(1)}, f32[5,3,4,8,128]{4,3,2,1,0:T(8,128)S(1)}, u32[]{:S(2)}, u32[]{:S(2)}) collective-permute-start(f32[5,3,4,8,128]{4,3,2,1,0:T(8,128)S(1)} %get-tuple-element.22), channel_id=1, source_target_pairs={{0,16},{16,0},{32,48},{48,32},{64,80},{80,64},{96,112},{112,96},{1... | collective-permute-start | bytes 737288 | tf_op jit(solution)/shard_map/ppermute | solution.py:310
  7.4 0.7 %collective-permute-start.1 = (f32[5,3,4,8,128]{4,3,2,1,0:T(8,128)S(1)}, f32[5,3,4,8,128]{4,3,2,1,0:T(8,128)S(1)}, u32[]{:S(2)}, u32[]{:S(2)}) collective-permute-start(f32[5,3,4,8,128]{4,3,2,1,0:T(8,128)S(1)} %get-tuple-element.23), channel_id=1, source_target_pairs={{0,240},{16,32},{32,16},{48,64},{64,48},{80,96},{96,80},{112,128},... | collective-permute-start | bytes 737288 | tf_op jit(solution)/shard_map/ppermute | solution.py:310
  8.2 4.4 %collective-permute-done.4.f_in = f32[5,3,4,8,128]{4,3,2,1,0:T(8,128)S(1)} collective-permute-done((f32[5,3,4,8,128]{4,3,2,1,0:T(8,128)S(1)}, f32[5,3,4,8,128]{4,3,2,1,0:T(8,128)S(1)}, u32[]{:S(2)}, u32[]{:S(2)}) %collective-permute-start.4) | collective-permute-done | bytes 245792 | tf_op jit(solution)/shard_map/ppermute | solution.py:310
  12.5 0.0 collective-permute-done.5.b_in
  12.5 0.9 %y0.1 = (f32[5,128,128]{2,1,0:T(8,128)S(1)}, f32[5,48,128]{2,1,0:T(8,128)S(1)}, f32[5,48,128]{2,1,0:T(8,128)S(1)}) custom-call(f32[5,4,4,8,128]{4,3,2,1,0:T(8,128)S(1)} %get-tuple-element.29.s_ref, f32[5,3,4,8,128]{4,3,2,1,0:T(8,128)S(1)} %collective-permute-done.4.f_in, f32[5,3,4,8,128]{4,3,2,1,0:T(8,128)S(1)} %collective-permute-done.5.b_in), custom_call_target="tpu_custom_call" | custom-call | flops 16384000 | bytes 1310720 | tf_op jit(solution)/shard_map/y0/pallas_call | solution.py:274
  13.5 2.7 %collective-permute-start.6 = (f32[5,48,128]{2,1,0:T(8,128)S(1)}, f32[5,48,128]{2,1,0:T(8,128)S(1)}, u32[]{:S(2)}, u32[]{:S(2)}) collective-permute-start(f32[5,48,128]{2,1,0:T(8,128)S(1)} %get-tuple-element.35), channel_id=1, source_target_pairs={{0,1},{1,0},{2,3},{3,2},{4,5},{5,4},{6,7},{7,6},{8,9},{9,8},{10,11... | collective-permute-start | bytes 368648 | tf_op jit(solution)/shard_map/ppermute | solution.py:314
  16.1 2.3 %collective-permute-start.7 = (f32[5,48,128]{2,1,0:T(8,128)S(1)}, f32[5,48,128]{2,1,0:T(8,128)S(1)}, u32[]{:S(2)}, u32[]{:S(2)}) collective-permute-start(f32[5,48,128]{2,1,0:T(8,128)S(1)} %get-tuple-element.36), channel_id=1, source_target_pairs={{0,15},{1,2},{2,1},{3,4},{4,3},{5,6},{6,5},{7,8},{8,7},{9,10},{10,... | collective-permute-start | bytes 368648 | tf_op jit(solution)/shard_map/ppermute | solution.py:314
  18.5 0.0 collective-permute-done.b
  18.5 0.0 collective-permute-done.1.f
  18.5 0.9 %y4.1 = (f32[5,128,128]{2,1,0:T(8,128)S(1)}, f32[5,48,128]{2,1,0:T(8,128)S(1)}, f32[5,48,128]{2,1,0:T(8,128)S(1)}) custom-call(f32[5,4,4,8,128]{4,3,2,1,0:T(8,128)S(1)} %get-tuple-element.21.s, f32[5,3,4,8,128]{4,3,2,1,0:T(8,128)S(1)} %collective-permute-done.b, f32[5,3,4,8,128]{4,3,2,1,0:T(8,128)S(1)} %collective-permute-done.1.f), custom_call_target="tpu_custom_call" | custom-call | flops 16384000 | bytes 1310720 | tf_op jit(solution)/shard_map/y4/pallas_call | solution.py:274
  19.4 4.5 %collective-permute-start.2 = (f32[5,48,128]{2,1,0:T(8,128)S(1)}, f32[5,48,128]{2,1,0:T(8,128)S(1)}, u32[]{:S(2)}, u32[]{:S(2)}) collective-permute-start(f32[5,48,128]{2,1,0:T(8,128)S(1)} %get-tuple-element.27), channel_id=1, source_target_pairs={{0,1},{1,0},{2,3},{3,2},{4,5},{5,4},{6,7},{7,6},{8,9},{9,8},{10,11... | collective-permute-start | bytes 368648 | tf_op jit(solution)/shard_map/ppermute | solution.py:314
  23.9 0.5 %collective-permute-start.3 = (f32[5,48,128]{2,1,0:T(8,128)S(1)}, f32[5,48,128]{2,1,0:T(8,128)S(1)}, u32[]{:S(2)}, u32[]{:S(2)}) collective-permute-start(f32[5,48,128]{2,1,0:T(8,128)S(1)} %get-tuple-element.28), channel_id=1, source_target_pairs={{0,15},{1,2},{2,1},{3,4},{4,3},{5,6},{6,5},{7,8},{8,7},{9,10},{10,... | collective-permute-start | bytes 368648 | tf_op jit(solution)/shard_map/ppermute | solution.py:314
  24.4 0.3 inner0.1
  24.7 0.3 inner4.1
  25.0 0.0 collective-permute-done.6.b
  25.0 0.0 collective-permute-done.7.f
  25.0 1.2 %z0.1._ = f32[5,8,32,128]{3,2,1,0:T(8,128)} custom-call(f32[5,128,128]{2,1,0:T(8,128)S(1)} %get-tuple-element.32.t_ref.t, f32[5,8,16,128]{3,2,1,0:T(8,128)S(1)} %get-tuple-element.33.q, f32[5,7,16,128]{3,2,1,0:T(8,128)S(1)} %get-tuple-element.34.mid, f32[5,48,128]{2,1,0:T(8,128)S(1)} %collective-permute-done.6.b, f32[5,48,128]{2,1,0:T(8,128)S(1)} %collective-permute-done.7.f), custom_call_target="tpu_custom_call" | custom-call | flops 11468800 | bytes 1310720 | tf_op jit(solution)/shard_map/z0/pallas_call | solution.py:295
  26.2 1.9 %collective-permute-done.2.b_in = f32[5,48,128]{2,1,0:T(8,128)S(1)} collective-permute-done((f32[5,48,128]{2,1,0:T(8,128)S(1)}, f32[5,48,128]{2,1,0:T(8,128)S(1)}, u32[]{:S(2)}, u32[]{:S(2)}) %collective-permute-start.2) | collective-permute-done | bytes 122912 | tf_op jit(solution)/shard_map/ppermute | solution.py:314
  28.1 3.1 %collective-permute-done.3.f_in = f32[5,48,128]{2,1,0:T(8,128)S(1)} collective-permute-done((f32[5,48,128]{2,1,0:T(8,128)S(1)}, f32[5,48,128]{2,1,0:T(8,128)S(1)}, u32[]{:S(2)}, u32[]{:S(2)}) %collective-permute-start.3) | collective-permute-done | bytes 122912 | tf_op jit(solution)/shard_map/ppermute | solution.py:314
  31.2 1.2 %z4.1 = f32[5,8,32,128]{3,2,1,0:T(8,128)} custom-call(f32[5,128,128]{2,1,0:T(8,128)S(1)} %get-tuple-element.24.t_ref, f32[5,8,16,128]{3,2,1,0:T(8,128)S(1)} %get-tuple-element.25.q_ref, f32[5,7,16,128]{3,2,1,0:T(8,128)S(1)} %get-tuple-element.26.mid_ref, f32[5,48,128]{2,1,0:T(8,128)S(1)} %collective-permute-done.2.b_in, ...), custom_call_target="tpu_custom_call", output_to_operand_aliasing={{}: (5, {})} | custom-call | flops 11468800 | bytes 1310720 | tf_op jit(solution)/shard_map/z4/pallas_call | solution.py:295
Async XLA Ops:
  2.4 10.2 %collective-permute-start.4 = (f32[5,3,4,8,128]{4,3,2,1,0:T(8,128)S(1)}, f32[5,3,4,8,128]{4,3,2,1,0:T(8,128)S(1)}, u32[]{:S(2)}, u32[]{:S(2)}) collective-permute-start(f32[5,3,4,8,128]{4,3,2,1,0:T(8,128)S(1)} %get-tuple-element.30), channel_id=1, source_target_pairs={{0,240},{16,32},{32,16},{48,64},{64,48},{80,96},{96,80},{112,128},... | collective-permute-start | bytes 737288 | tf_op jit(solution)/shard_map/ppermute | solution.py:310
  5.6 7.0 %collective-permute-start.5 = (f32[5,3,4,8,128]{4,3,2,1,0:T(8,128)S(1)}, f32[5,3,4,8,128]{4,3,2,1,0:T(8,128)S(1)}, u32[]{:S(2)}, u32[]{:S(2)}) collective-permute-start(f32[5,3,4,8,128]{4,3,2,1,0:T(8,128)S(1)} %get-tuple-element.31), channel_id=1, source_target_pairs={{0,16},{16,0},{32,48},{48,32},{64,80},{80,64},{96,112},{112,96},{1... | collective-permute-start | bytes 737288 | tf_op jit(solution)/shard_map/ppermute | solution.py:310
  6.8 11.6 %collective-permute-start = (f32[5,3,4,8,128]{4,3,2,1,0:T(8,128)S(1)}, f32[5,3,4,8,128]{4,3,2,1,0:T(8,128)S(1)}, u32[]{:S(2)}, u32[]{:S(2)}) collective-permute-start(f32[5,3,4,8,128]{4,3,2,1,0:T(8,128)S(1)} %get-tuple-element.22), channel_id=1, source_target_pairs={{0,16},{16,0},{32,48},{48,32},{64,80},{80,64},{96,112},{112,96},{1... | collective-permute-start | bytes 737288 | tf_op jit(solution)/shard_map/ppermute | solution.py:310
  7.4 11.0 %collective-permute-start.1 = (f32[5,3,4,8,128]{4,3,2,1,0:T(8,128)S(1)}, f32[5,3,4,8,128]{4,3,2,1,0:T(8,128)S(1)}, u32[]{:S(2)}, u32[]{:S(2)}) collective-permute-start(f32[5,3,4,8,128]{4,3,2,1,0:T(8,128)S(1)} %get-tuple-element.23), channel_id=1, source_target_pairs={{0,240},{16,32},{32,16},{48,64},{64,48},{80,96},{96,80},{112,128},... | collective-permute-start | bytes 737288 | tf_op jit(solution)/shard_map/ppermute | solution.py:310
  13.5 11.5 %collective-permute-start.6 = (f32[5,48,128]{2,1,0:T(8,128)S(1)}, f32[5,48,128]{2,1,0:T(8,128)S(1)}, u32[]{:S(2)}, u32[]{:S(2)}) collective-permute-start(f32[5,48,128]{2,1,0:T(8,128)S(1)} %get-tuple-element.35), channel_id=1, source_target_pairs={{0,1},{1,0},{2,3},{3,2},{4,5},{5,4},{6,7},{7,6},{8,9},{9,8},{10,11... | collective-permute-start | bytes 368648 | tf_op jit(solution)/shard_map/ppermute | solution.py:314
  16.1 8.8 %collective-permute-start.7 = (f32[5,48,128]{2,1,0:T(8,128)S(1)}, f32[5,48,128]{2,1,0:T(8,128)S(1)}, u32[]{:S(2)}, u32[]{:S(2)}) collective-permute-start(f32[5,48,128]{2,1,0:T(8,128)S(1)} %get-tuple-element.36), channel_id=1, source_target_pairs={{0,15},{1,2},{2,1},{3,4},{4,3},{5,6},{6,5},{7,8},{8,7},{9,10},{10,... | collective-permute-start | bytes 368648 | tf_op jit(solution)/shard_map/ppermute | solution.py:314
  19.4 8.7 %collective-permute-start.2 = (f32[5,48,128]{2,1,0:T(8,128)S(1)}, f32[5,48,128]{2,1,0:T(8,128)S(1)}, u32[]{:S(2)}, u32[]{:S(2)}) collective-permute-start(f32[5,48,128]{2,1,0:T(8,128)S(1)} %get-tuple-element.27), channel_id=1, source_target_pairs={{0,1},{1,0},{2,3},{3,2},{4,5},{5,4},{6,7},{7,6},{8,9},{9,8},{10,11... | collective-permute-start | bytes 368648 | tf_op jit(solution)/shard_map/ppermute | solution.py:314
  23.9 7.3 %collective-permute-start.3 = (f32[5,48,128]{2,1,0:T(8,128)S(1)}, f32[5,48,128]{2,1,0:T(8,128)S(1)}, u32[]{:S(2)}, u32[]{:S(2)}) collective-permute-start(f32[5,48,128]{2,1,0:T(8,128)S(1)} %get-tuple-element.28), channel_id=1, source_target_pairs={{0,15},{1,2},{2,1},{3,4},{4,3},{5,6},{6,5},{7,8},{8,7},{9,10},{10,... | collective-permute-start | bytes 368648 | tf_op jit(solution)/shard_map/ppermute | solution.py:314
